TPU v7x, 32 devices: a whole 2x2x4 slice. The times are simulated.
32 devices in a mesh: dp: 8 (over y, x, core), fsdp: 4 (over z).
Axes of the slice: x: 2, y: 2, z: 4, core: 2. Of those that a mesh axis runs over, the one named last changes fastest.
Arguments:
- latent: bfloat16 [16, 1024, 1408], P('dp', 'fsdp'), may hold values from -6 to 6
- skip_state: bfloat16 [16, 1024, 1408], P('dp', 'fsdp'), may hold values from -6 to 6
- text_states: bfloat16 [16, 333, 1024], P('dp', None, 'fsdp'), may hold values from -6 to 6
- timestep: int32 [16], P('dp'), may hold values from 0 to 999
- position_grid: int32 [16, 2, 1024], P('dp', None, 'fsdp'), may hold values from 0 to 63, as said below
- cotangent: bfloat16 [16, 1024, 1408], P('dp', 'fsdp'), may hold values from -6 to 6
- skip_gain: float32 [2816], replicated, may hold values from 0.5 to 1.5
- skip_bias: float32 [2816], replicated, may hold values from -1 to 1
- skip_w: bfloat16 [2816, 1408], P('dp', 'fsdp'), may hold values from -0.109375 to 0.109375
- skip_b: float32 [1408], replicated, may hold values from -1 to 1
- ada_w: bfloat16 [1408, 1408], P('dp', 'fsdp'), may hold values from -0.15625 to 0.15625
- ada_b: float32 [1408], replicated, may hold values from -1 to 1
- norm1_gain: float32 [1408], replicated, may hold values from 0.5 to 1.5
- norm1_bias: float32 [1408], replicated, may hold values from -1 to 1
- qkv_w: bfloat16 [1408, 4224], P('dp', 'fsdp'), may hold values from -0.15625 to 0.15625
- qkv_b: float32 [4224], replicated, may hold values from -1 to 1
- qnorm1_gain: float32 [88], replicated, may hold values from 0.5 to 1.5
- qnorm1_bias: float32 [88], replicated, may hold values from -1 to 1
- knorm1_gain: float32 [88], replicated, may hold values from 0.5 to 1.5
- knorm1_bias: float32 [88], replicated, may hold values from -1 to 1
- proj1_w: bfloat16 [1408, 1408], P('dp', 'fsdp'), may hold values from -2.5 to 2.5
- proj1_b: float32 [1408], replicated, may hold values from -1 to 1
- norm3_gain: float32 [1408], replicated, may hold values from 0.5 to 1.5
- norm3_bias: float32 [1408], replicated, may hold values from -1 to 1
- q2_w: bfloat16 [1408, 1408], P('dp', 'fsdp'), may hold values from -0.15625 to 0.15625
- q2_b: float32 [1408], replicated, may hold values from -1 to 1
- kv2_w: bfloat16 [2816, 1024], P('dp', 'fsdp'), may hold values from -0.1875 to 0.1875
- kv2_b: float32 [2816], replicated, may hold values from -1 to 1
- qnorm2_gain: float32 [88], replicated, may hold values from 0.5 to 1.5
- qnorm2_bias: float32 [88], replicated, may hold values from -1 to 1
- knorm2_gain: float32 [88], replicated, may hold values from 0.5 to 1.5
- proj2_w: bfloat16 [1408, 1408], P('dp', 'fsdp'), may hold values from -2 to 2
- proj2_b: float32 [1408], replicated, may hold values from -1 to 1
- norm2_gain: float32 [1408], replicated, may hold values from 0.5 to 1.5
- norm2_bias: float32 [1408], replicated, may hold values from -1 to 1
- fc1_w: bfloat16 [1408, 6144], P('dp', 'fsdp'), may hold values from -0.15625 to 0.15625
- fc1_b: float32 [6144], replicated, may hold values from -1 to 1
- fc2_w: bfloat16 [6144, 1408], P('dp', 'fsdp'), may hold values from -0.078125 to 0.078125
- fc2_b: float32 [1408], replicated, may hold values from -1 to 1
Outputs:
- block_out: bfloat16 [16, 1024, 1408], P('dp', 'fsdp')
- latent_grad: float32 [16, 1024, 1408], P('dp', 'fsdp')
- skip_grad: float32 [16, 1024, 1408], P('dp', 'fsdp')
- text_grad: float32 [16, 333, 1024], P('dp', None, 'fsdp')
- skip_gain_grad: float32 [2816], replicated
- skip_bias_grad: float32 [2816], replicated
- skip_w_grad: float32 [2816, 1408], P('dp', 'fsdp')
- skip_b_grad: float32 [1408], replicated
- ada_w_grad: float32 [1408, 1408], P('dp', 'fsdp')
- ada_b_grad: float32 [1408], replicated
- norm1_gain_grad: float32 [1408], replicated
- norm1_bias_grad: float32 [1408], replicated
- qkv_w_grad: float32 [1408, 4224], P('dp', 'fsdp')
- qkv_b_grad: float32 [4224], replicated
- qnorm1_gain_grad: float32 [88], replicated
- qnorm1_bias_grad: float32 [88], replicated
- knorm1_gain_grad: float32 [88], replicated
- knorm1_bias_grad: float32 [88], replicated
- proj1_w_grad: float32 [1408, 1408], P('dp', 'fsdp')
- proj1_b_grad: float32 [1408], replicated
- norm3_gain_grad: float32 [1408], replicated
- norm3_bias_grad: float32 [1408], replicated
- q2_w_grad: float32 [1408, 1408], P('dp', 'fsdp')
- q2_b_grad: float32 [1408], replicated
- kv2_w_grad: float32 [2816, 1024], P('dp', 'fsdp')
- kv2_b_grad: float32 [2816], replicated
- qnorm2_gain_grad: float32 [88], replicated
- qnorm2_bias_grad: float32 [88], replicated
- knorm2_gain_grad: float32 [88], replicated
- proj2_w_grad: float32 [1408, 1408], P('dp', 'fsdp')
- proj2_b_grad: float32 [1408], replicated
- norm2_gain_grad: float32 [1408], replicated
- norm2_bias_grad: float32 [1408], replicated
- fc1_w_grad: float32 [1408, 6144], P('dp', 'fsdp')
- fc1_b_grad: float32 [6144], replicated
- fc2_w_grad: float32 [6144, 1408], P('dp', 'fsdp')
- fc2_b_grad: float32 [1408], replicated
Inputs may be any that keep to these rules, and one draw needn't show every extreme that they name: `position_grid`: in each sequence, token i along the last dimension has row i // W in entry 0 and column i mod W in entry 1, for a power of two W of that sequence that divides 1024; the first sequence has the narrowest grid.
All inputs are finite; a program needn't handle non-finite values.
Results may differ from a plain program's by a relative error of at most 0.028.
Values may be sent and summed in bfloat16 or wider, within the bound.
No kernel may reach another device: no remote copies, remote signals or barrier semaphores. Data moves between devices by JAX's collectives and lax.ppermute only.
A program may use at most 384 MiB of HBM per device.

v0:
```python
from functools import partial
import math

import jax
import jax.numpy as jnp
from jax import lax
from jax.sharding import PartitionSpec as P

norm_eps = 1e-06
head_group = 4


def layer_norm(values, norm_gain, norm_bias):
    center = values - jnp.mean(values, axis=-1, keepdims=True)
    spread = jnp.mean(center * center, axis=-1, keepdims=True)
    return center * lax.rsqrt(spread + norm_eps) * norm_gain + norm_bias


def rotary(position_grid, values):
    quarter = values.shape[-1] // 4
    frequency = jnp.exp(jnp.arange(quarter, dtype=jnp.float32) * (-math.log(10000.0) / quarter))
    row_angle = position_grid[:, 0, :, None].astype(jnp.float32) * frequency
    col_angle = position_grid[:, 1, :, None].astype(jnp.float32) * frequency
    angles = jnp.concatenate([row_angle, row_angle, col_angle, col_angle], axis=-1)[:, :, None, :]
    pieces = jnp.split(values, 4, axis=-1)
    turned = jnp.concatenate([-pieces[1], pieces[0], -pieces[3], pieces[2]], axis=-1)
    return values * jnp.cos(angles) + turned * jnp.sin(angles)


def time_embedding(timestep, model_width):
    halfway = model_width // 2
    frequency = jnp.exp(jnp.arange(halfway, dtype=jnp.float32) * (-math.log(10000.0) / halfway))
    angles = timestep.astype(jnp.float32)[:, None] * frequency
    return jnp.concatenate([jnp.cos(angles), jnp.sin(angles)], axis=-1)


def self_heads(position_grid, qkv_rows, qnorm_gain, qnorm_bias, knorm_gain, knorm_bias):
    head_size = qnorm_gain.shape[0]
    shaped = qkv_rows.reshape(qkv_rows.shape[:2] + (3, -1, head_size))
    queries = rotary(
        position_grid, layer_norm(shaped[:, :, 0], qnorm_gain, qnorm_bias)
    ) * head_size ** (-0.5)
    key_rows = rotary(position_grid, layer_norm(shaped[:, :, 1], knorm_gain, knorm_bias))
    return (queries, key_rows, shaped[:, :, 2])


def cross_queries(position_grid, projected, qnorm_gain, qnorm_bias):
    head_size = qnorm_gain.shape[0]
    shaped = projected.reshape(projected.shape[:2] + (-1, head_size))
    return rotary(position_grid, layer_norm(shaped, qnorm_gain, qnorm_bias)) * head_size ** (-0.5)


def cross_keys(text_kv, knorm_gain):
    head_size = knorm_gain.shape[0]
    half_width = text_kv.shape[-1] // 2
    key_part = text_kv[..., :half_width].reshape(text_kv.shape[:2] + (-1, head_size))
    value_part = text_kv[..., half_width:].reshape(text_kv.shape[:2] + (-1, head_size))
    return (layer_norm(key_part, knorm_gain, jnp.zeros_like(knorm_gain)), value_part)


def gelu_tanh(pre_values):
    return jax.nn.gelu(pre_values, approximate=True)


def project(inputs, weight):
    return jnp.dot(inputs, weight, preferred_element_type=jnp.float32)


def project_back(grad_low, weight):
    return lax.dot_general(
        grad_low,
        weight,
        (((grad_low.ndim - 1,), (1,)), ((), ())),
        preferred_element_type=jnp.float32,
    )


def weight_grad(inputs, grad_low):
    flat_in = inputs.reshape(-1, inputs.shape[-1])
    flat_grad = grad_low.reshape(-1, grad_low.shape[-1])
    return lax.dot_general(
        flat_in, flat_grad, (((0,), (0,)), ((), ())), preferred_element_type=jnp.float32
    )


def column_sum(grad_low):
    return jnp.sum(grad_low.reshape(-1, grad_low.shape[-1]), axis=0, dtype=jnp.float32)


def attend_forward(queries, key_rows, values):
    seq_count, query_len, head_count, head_size = queries.shape

    def one_group(group_index, state_pair):
        outputs, lse_all = state_pair
        first_head = group_index * head_group
        query_part = lax.dynamic_slice_in_dim(queries, first_head, head_group, 2)
        key_part = lax.dynamic_slice_in_dim(key_rows, first_head, head_group, 2)
        value_part = lax.dynamic_slice_in_dim(values, first_head, head_group, 2)
        scores = jnp.einsum(
            "sqhd,skhd->shqk", query_part, key_part, preferred_element_type=jnp.float32
        )
        row_max = jnp.max(scores, axis=-1, keepdims=True)
        row_total = jnp.sum(jnp.exp(scores - row_max), axis=-1, keepdims=True)
        log_total = row_max + jnp.log(row_total)
        probabilities = jnp.exp(scores - log_total).astype(jnp.bfloat16)
        result = jnp.einsum(
            "shqk,skhd->sqhd", probabilities, value_part, preferred_element_type=jnp.float32
        )
        outputs = lax.dynamic_update_slice_in_dim(outputs, result, first_head, 2)
        lse_all = lax.dynamic_update_slice_in_dim(lse_all, log_total[..., 0], first_head, 1)
        return (outputs, lse_all)

    outputs = jnp.zeros(queries.shape, jnp.float32)
    lse_all = jnp.zeros((seq_count, head_count, query_len), jnp.float32)
    return lax.fori_loop(0, head_count // head_group, one_group, (outputs, lse_all))


def attend_backward(queries, key_rows, values, lse_all, grad_low):
    head_count = queries.shape[2]

    def one_group(group_index, state_triple):
        grad_query, grad_key, grad_value = state_triple
        first_head = group_index * head_group
        query_part = lax.dynamic_slice_in_dim(queries, first_head, head_group, 2)
        key_part = lax.dynamic_slice_in_dim(key_rows, first_head, head_group, 2)
        value_part = lax.dynamic_slice_in_dim(values, first_head, head_group, 2)
        grad_part = lax.dynamic_slice_in_dim(grad_low, first_head, head_group, 2)
        lse_part = lax.dynamic_slice_in_dim(lse_all, first_head, head_group, 1)
        scores = jnp.einsum(
            "sqhd,skhd->shqk", query_part, key_part, preferred_element_type=jnp.float32
        )
        probabilities = jnp.exp(scores - lse_part[..., None])
        grad_prob = jnp.einsum(
            "sqhd,skhd->shqk", grad_part, value_part, preferred_element_type=jnp.float32
        )
        grad_score = probabilities * (
            grad_prob - jnp.sum(probabilities * grad_prob, axis=-1, keepdims=True)
        )
        grad_score = grad_score.astype(jnp.bfloat16)
        dq_part = jnp.einsum(
            "shqk,skhd->sqhd", grad_score, key_part, preferred_element_type=jnp.float32
        )
        dk_part = jnp.einsum(
            "shqk,sqhd->skhd", grad_score, query_part, preferred_element_type=jnp.float32
        )
        dv_part = jnp.einsum(
            "shqk,sqhd->skhd",
            probabilities.astype(jnp.bfloat16),
            grad_part,
            preferred_element_type=jnp.float32,
        )
        grad_query = lax.dynamic_update_slice_in_dim(grad_query, dq_part, first_head, 2)
        grad_key = lax.dynamic_update_slice_in_dim(grad_key, dk_part, first_head, 2)
        grad_value = lax.dynamic_update_slice_in_dim(grad_value, dv_part, first_head, 2)
        return (grad_query, grad_key, grad_value)

    initial = (
        jnp.zeros(queries.shape, jnp.float32),
        jnp.zeros(key_rows.shape, jnp.float32),
        jnp.zeros(values.shape, jnp.float32),
    )
    return lax.fori_loop(0, head_count // head_group, one_group, initial)


def gather_columns(matrices):
    return (
        lax.all_gather(matrices[0], "fsdp", axis=1, tiled=True),
        lax.all_gather(matrices[1], "fsdp", axis=1, tiled=True),
        lax.all_gather(matrices[2], "fsdp", axis=1, tiled=True),
        lax.all_gather(matrices[3], "fsdp", axis=1, tiled=True),
        lax.all_gather(matrices[4], "fsdp", axis=1, tiled=True),
        lax.all_gather(matrices[5], "fsdp", axis=1, tiled=True),
        lax.all_gather(matrices[6], "fsdp", axis=1, tiled=True),
        lax.all_gather(matrices[7], "fsdp", axis=1, tiled=True),
    )


def gather_rows(matrices, text_weight):
    gathered = (
        lax.all_gather(matrices[0], "dp", axis=0, tiled=True),
        lax.all_gather(matrices[1], "dp", axis=0, tiled=True),
        lax.all_gather(matrices[2], "dp", axis=0, tiled=True),
        lax.all_gather(matrices[3], "dp", axis=0, tiled=True),
        lax.all_gather(matrices[4], "dp", axis=0, tiled=True),
        lax.all_gather(matrices[5], "dp", axis=0, tiled=True),
        lax.all_gather(matrices[6], "dp", axis=0, tiled=True),
        lax.all_gather(matrices[7], "dp", axis=0, tiled=True),
        lax.all_gather(text_weight, "dp", axis=0, tiled=True),
    )
    return (gathered[:8], gathered[8])


def fetch_weights(matrices, text_weight):
    return gather_rows(gather_columns(matrices), text_weight)


def reduce_columns(gradients):
    return (
        lax.psum_scatter(
            gradients[0].astype(jnp.bfloat16), "fsdp", scatter_dimension=1, tiled=True
        ).astype(jnp.float32),
        lax.psum_scatter(
            gradients[1].astype(jnp.bfloat16), "fsdp", scatter_dimension=1, tiled=True
        ).astype(jnp.float32),
        lax.psum_scatter(
            gradients[2].astype(jnp.bfloat16), "fsdp", scatter_dimension=1, tiled=True
        ).astype(jnp.float32),
        lax.psum_scatter(
            gradients[3].astype(jnp.bfloat16), "fsdp", scatter_dimension=1, tiled=True
        ).astype(jnp.float32),
        lax.psum_scatter(
            gradients[4].astype(jnp.bfloat16), "fsdp", scatter_dimension=1, tiled=True
        ).astype(jnp.float32),
        lax.psum_scatter(
            gradients[5].astype(jnp.bfloat16), "fsdp", scatter_dimension=1, tiled=True
        ).astype(jnp.float32),
        lax.psum_scatter(
            gradients[6].astype(jnp.bfloat16), "fsdp", scatter_dimension=1, tiled=True
        ).astype(jnp.float32),
        lax.psum_scatter(
            gradients[7].astype(jnp.bfloat16), "fsdp", scatter_dimension=1, tiled=True
        ).astype(jnp.float32),
    )


def reduce_rows(gradients, text_part):
    summed = (
        lax.psum_scatter(gradients[0], "dp", scatter_dimension=0, tiled=True),
        lax.psum_scatter(gradients[1], "dp", scatter_dimension=0, tiled=True),
        lax.psum_scatter(gradients[2], "dp", scatter_dimension=0, tiled=True),
        lax.psum_scatter(gradients[3], "dp", scatter_dimension=0, tiled=True),
        lax.psum_scatter(gradients[4], "dp", scatter_dimension=0, tiled=True),
        lax.psum_scatter(gradients[5], "dp", scatter_dimension=0, tiled=True),
        lax.psum_scatter(gradients[6], "dp", scatter_dimension=0, tiled=True),
        lax.psum_scatter(gradients[7], "dp", scatter_dimension=0, tiled=True),
        lax.psum_scatter(text_part, "dp", scatter_dimension=0, tiled=True),
    )
    return (summed[:8], summed[8])


def reduce_weights(gradients, text_part):
    row_part, text_done = reduce_rows(gradients, text_part)
    return (reduce_columns(row_part), text_done)


def body(
    latent,
    skip_state,
    text_states,
    timestep,
    position_grid,
    cotangent,
    skip_gain,
    skip_bias,
    skip_w,
    skip_b,
    ada_w,
    ada_b,
    norm1_gain,
    norm1_bias,
    qkv_w,
    qkv_b,
    qnorm1_gain,
    qnorm1_bias,
    knorm1_gain,
    knorm1_bias,
    proj1_w,
    proj1_b,
    norm3_gain,
    norm3_bias,
    q2_w,
    q2_b,
    kv2_w,
    kv2_b,
    qnorm2_gain,
    qnorm2_bias,
    knorm2_gain,
    proj2_w,
    proj2_b,
    norm2_gain,
    norm2_bias,
    fc1_w,
    fc1_b,
    fc2_w,
    fc2_b,
):
    seq_count, row_count, model_width = latent.shape
    head_size = qnorm1_gain.shape[0]
    head_count = model_width // head_size
    shards = (skip_w, ada_w, qkv_w, proj1_w, q2_w, proj2_w, fc1_w, fc2_w)
    matrices, text_weight = fetch_weights(shards, kv2_w)
    w_skip, w_ada, w_qkv, w_proj1, w_q2, w_proj2, w_fc1, w_fc2 = matrices
    joined_in = jnp.concatenate([latent, skip_state], axis=-1).astype(jnp.float32)
    joined = layer_norm(joined_in, skip_gain, skip_bias).astype(jnp.bfloat16)
    resid_one = project(joined, w_skip) + skip_b
    embed_act = jax.nn.silu(time_embedding(timestep, model_width)).astype(jnp.bfloat16)
    shift = project(embed_act, w_ada) + ada_b
    normed = (layer_norm(resid_one, norm1_gain, norm1_bias) + shift[:, None, :]).astype(
        jnp.bfloat16
    )
    qkv_rows = project(normed, w_qkv) + qkv_b
    queries, key_rows, value_rows = self_heads(
        position_grid, qkv_rows, qnorm1_gain, qnorm1_bias, knorm1_gain, knorm1_bias
    )
    queries_low = queries.astype(jnp.bfloat16)
    key_low = key_rows.astype(jnp.bfloat16).reshape(seq_count, row_count, model_width)
    value_low = value_rows.astype(jnp.bfloat16).reshape(seq_count, row_count, model_width)
    key_all, value_all = (
        lax.all_gather(key_low, "fsdp", axis=1, tiled=True),
        lax.all_gather(value_low, "fsdp", axis=1, tiled=True),
    )
    key_all = key_all.reshape(seq_count, -1, head_count, head_size)
    value_all = value_all.reshape(seq_count, -1, head_count, head_size)
    mixed, self_lse = attend_forward(queries_low, key_all, value_all)
    mixed_low = mixed.reshape(seq_count, row_count, model_width).astype(jnp.bfloat16)
    resid_two = resid_one + project(mixed_low, w_proj1) + proj1_b
    cross_in = layer_norm(resid_two, norm3_gain, norm3_bias).astype(jnp.bfloat16)
    cross_proj = project(cross_in, w_q2) + q2_b
    cross_q = cross_queries(position_grid, cross_proj, qnorm2_gain, qnorm2_bias).astype(
        jnp.bfloat16
    )
    text_part = jnp.einsum(
        "stc,ec->ste", text_states, text_weight, preferred_element_type=jnp.float32
    )
    text_kv = lax.psum(text_part, "fsdp") + kv2_b
    cross_k, cross_v = cross_keys(text_kv, knorm2_gain)
    cross_k_low = cross_k.astype(jnp.bfloat16)
    cross_v_low = cross_v.astype(jnp.bfloat16)
    cross_mixed, cross_lse = attend_forward(cross_q, cross_k_low, cross_v_low)
    cross_low = cross_mixed.reshape(seq_count, row_count, model_width).astype(jnp.bfloat16)
    resid_three = resid_two + project(cross_low, w_proj2) + proj2_b
    ffn_in = layer_norm(resid_three, norm2_gain, norm2_bias).astype(jnp.bfloat16)
    pre_act = project(ffn_in, w_fc1) + fc1_b
    hidden = gelu_tanh(pre_act).astype(jnp.bfloat16)
    block_out = (resid_three + project(hidden, w_fc2) + fc2_b).astype(jnp.bfloat16)
    matrices, text_weight = fetch_weights(shards, kv2_w)
    w_skip, w_ada, w_qkv, w_proj1, w_q2, w_proj2, w_fc1, w_fc2 = matrices
    grad_out = cotangent.astype(jnp.float32)
    grad_fc2 = weight_grad(hidden, cotangent)
    bias_fc2 = column_sum(cotangent)
    grad_hidden = project_back(cotangent, w_fc2)
    grad_pre = jax.vjp(gelu_tanh, pre_act)[1](grad_hidden)[0].astype(jnp.bfloat16)
    grad_fc1 = weight_grad(ffn_in, grad_pre)
    bias_fc1 = column_sum(grad_pre)
    grad_ffn_in = project_back(grad_pre, w_fc1)
    grad_resid3, gain_n2, bias_n2 = jax.vjp(layer_norm, resid_three, norm2_gain, norm2_bias)[1](
        grad_ffn_in
    )
    grad_resid3 = grad_resid3 + grad_out
    grad_branch2 = grad_resid3.astype(jnp.bfloat16)
    grad_proj2 = weight_grad(cross_low, grad_branch2)
    bias_proj2 = column_sum(grad_branch2)
    grad_cross = project_back(grad_branch2, w_proj2).astype(jnp.bfloat16)
    grad_cross = grad_cross.reshape(seq_count, row_count, head_count, head_size)
    grad_cq, grad_ck, grad_cv = attend_backward(
        cross_q, cross_k_low, cross_v_low, cross_lse, grad_cross
    )
    grad_text_kv, gain_kn2 = jax.vjp(cross_keys, text_kv, knorm2_gain)[1]((grad_ck, grad_cv))
    text_sum = lax.psum(grad_text_kv.astype(jnp.bfloat16), "fsdp")
    grad_kv2 = weight_grad(text_sum, text_states)
    bias_kv2 = column_sum(text_sum) / lax.axis_size("fsdp")
    text_grad = jnp.einsum("ste,ec->stc", text_sum, text_weight, preferred_element_type=jnp.float32)
    grad_cproj, gain_qn2, bias_qn2 = jax.vjp(
        partial(cross_queries, position_grid), cross_proj, qnorm2_gain, qnorm2_bias
    )[1](grad_cq)
    grad_cproj = grad_cproj.astype(jnp.bfloat16)
    grad_q2 = weight_grad(cross_in, grad_cproj)
    bias_q2 = column_sum(grad_cproj)
    grad_cross_in = project_back(grad_cproj, w_q2)
    grad_resid2, gain_n3, bias_n3 = jax.vjp(layer_norm, resid_two, norm3_gain, norm3_bias)[1](
        grad_cross_in
    )
    grad_resid2 = grad_resid2 + grad_resid3
    grad_branch1 = grad_resid2.astype(jnp.bfloat16)
    grad_proj1 = weight_grad(mixed_low, grad_branch1)
    bias_proj1 = column_sum(grad_branch1)
    grad_mixed = project_back(grad_branch1, w_proj1).astype(jnp.bfloat16)
    grad_mixed = grad_mixed.reshape(seq_count, row_count, head_count, head_size)
    grad_sq, grad_sk, grad_sv = attend_backward(
        queries_low, key_all, value_all, self_lse, grad_mixed
    )
    own_key, own_value = (
        lax.psum_scatter(
            grad_sk.reshape(seq_count, -1, model_width).astype(jnp.bfloat16),
            "fsdp",
            scatter_dimension=1,
            tiled=True,
        ).astype(jnp.float32),
        lax.psum_scatter(
            grad_sv.reshape(seq_count, -1, model_width).astype(jnp.bfloat16),
            "fsdp",
            scatter_dimension=1,
            tiled=True,
        ).astype(jnp.float32),
    )
    own_key = own_key.reshape(seq_count, row_count, head_count, head_size)
    own_value = own_value.reshape(seq_count, row_count, head_count, head_size)
    grad_qkv, gain_qn1, bias_qn1, gain_kn1, bias_kn1 = jax.vjp(
        partial(self_heads, position_grid),
        qkv_rows,
        qnorm1_gain,
        qnorm1_bias,
        knorm1_gain,
        knorm1_bias,
    )[1]((grad_sq, own_key, own_value))
    grad_qkv = grad_qkv.astype(jnp.bfloat16)
    grad_qkv_w = weight_grad(normed, grad_qkv)
    bias_qkv = column_sum(grad_qkv)
    grad_normed = project_back(grad_qkv, w_qkv)
    grad_shift = jnp.sum(grad_normed, axis=1)
    grad_ada = lax.dot_general(
        embed_act.astype(jnp.float32),
        grad_shift,
        (((0,), (0,)), ((), ())),
        precision=lax.Precision.HIGHEST,
    )
    bias_ada = jnp.sum(grad_shift, axis=0)
    grad_resid1, gain_n1, bias_n1 = jax.vjp(layer_norm, resid_one, norm1_gain, norm1_bias)[1](
        grad_normed
    )
    grad_resid1 = (grad_resid1 + grad_resid2).astype(jnp.bfloat16)
    grad_skip_w = weight_grad(joined, grad_resid1)
    bias_skip = column_sum(grad_resid1)
    grad_joined = project_back(grad_resid1, w_skip)
    grad_cat, gain_skip, bias_skip_norm = jax.vjp(layer_norm, joined_in, skip_gain, skip_bias)[1](
        grad_joined
    )
    latent_grad = grad_cat[..., :model_width]
    skip_grad = grad_cat[..., model_width:]
    vectors = lax.psum(
        (
            gain_skip,
            bias_skip_norm,
            bias_skip,
            bias_ada,
            gain_n1,
            bias_n1,
            bias_qkv,
            gain_qn1,
            bias_qn1,
            gain_kn1,
            bias_kn1,
            bias_proj1,
            gain_n3,
            bias_n3,
            bias_q2,
            bias_kv2,
            gain_qn2,
            bias_qn2,
            gain_kn2,
            bias_proj2,
            gain_n2,
            bias_n2,
            bias_fc1,
            bias_fc2,
        ),
        ("dp", "fsdp"),
    )
    reduced, kv_grad = reduce_weights(
        (grad_skip_w, grad_ada, grad_qkv_w, grad_proj1, grad_q2, grad_proj2, grad_fc1, grad_fc2),
        grad_kv2,
    )
    return (
        block_out,
        latent_grad,
        skip_grad,
        text_grad,
        vectors[0],
        vectors[1],
        reduced[0],
        vectors[2],
        reduced[1],
        vectors[3],
        vectors[4],
        vectors[5],
        reduced[2],
        vectors[6],
        vectors[7],
        vectors[8],
        vectors[9],
        vectors[10],
        reduced[3],
        vectors[11],
        vectors[12],
        vectors[13],
        reduced[4],
        vectors[14],
        kv_grad,
        vectors[15],
        vectors[16],
        vectors[17],
        vectors[18],
        reduced[5],
        vectors[19],
        vectors[20],
        vectors[21],
        reduced[6],
        vectors[22],
        reduced[7],
        vectors[23],
    )


def solution(mesh):
    in_specs = (
        P("dp", "fsdp", None),
        P("dp", "fsdp", None),
        P("dp", None, "fsdp"),
        P("dp"),
        P("dp", None, "fsdp"),
        P("dp", "fsdp", None),
        P(),
        P(),
        P("dp", "fsdp"),
        P(),
        P("dp", "fsdp"),
        P(),
        P(),
        P(),
        P("dp", "fsdp"),
        P(),
        P(),
        P(),
        P(),
        P(),
        P("dp", "fsdp"),
        P(),
        P(),
        P(),
        P("dp", "fsdp"),
        P(),
        P("dp", "fsdp"),
        P(),
        P(),
        P(),
        P(),
        P("dp", "fsdp"),
        P(),
        P(),
        P(),
        P("dp", "fsdp"),
        P(),
        P("dp", "fsdp"),
        P(),
    )
    out_specs = (
        P("dp", "fsdp", None),
        P("dp", "fsdp", None),
        P("dp", "fsdp", None),
        P("dp", None, "fsdp"),
        P(),
        P(),
        P("dp", "fsdp"),
        P(),
        P("dp", "fsdp"),
        P(),
        P(),
        P(),
        P("dp", "fsdp"),
        P(),
        P(),
        P(),
        P(),
        P(),
        P("dp", "fsdp"),
        P(),
        P(),
        P(),
        P("dp", "fsdp"),
        P(),
        P("dp", "fsdp"),
        P(),
        P(),
        P(),
        P(),
        P("dp", "fsdp"),
        P(),
        P(),
        P(),
        P("dp", "fsdp"),
        P(),
        P("dp", "fsdp"),
        P(),
    )
    return jax.shard_map(body, mesh=mesh, in_specs=in_specs, out_specs=out_specs, check_vma=False)
```

profile of v0, /device:TPU:0, one launch (start us, length us, event | category | flops | bytes accessed | tf_op | source)
XLA Modules:
  0.0 3206.3 jit_solution(16720829113566558233)
XLA Ops:
  136.8 52.0 %all-gather.20.cloned.1.call-done = bf16[2816,1408]{1,0:T(8,128)(2,1)} async-done(((bf16[352,1408]{1,0:T(8,128)(2,1)}), bf16[2816,1408]{1,0:T(8,128)(2,1)}) %all-gather.20.cloned.1.call-update) | async-done | bytes 7929872 | tf_op jit(solution)/shard_map/all_gather | solution.py:180
  198.8 61.6 %all-gather.24.cloned.1.call-done = bf16[1408,4224]{1,0:T(8,128)(2,1)} async-done(((bf16[176,4224]{1,0:T(8,128)(2,1)}), bf16[1408,4224]{1,0:T(8,128)(2,1)}) %all-gather.24.cloned.1.call-update) | async-done | bytes 11894800 | tf_op jit(solution)/shard_map/all_gather | solution.py:182
  380.1 262.1 %all-reduce.10.cloned.1.call-done = f32[2,333,2816]{2,1,0:T(8,128)} async-done(((f32[2,333,2816]{2,1,0:T(8,128)}), f32[2,333,2816]{2,1,0:T(8,128)}) %all-reduce.10.cloned.1.call-update) | async-done | bytes 7501840 | tf_op jit(solution)/shard_map/psum | solution.py:325
  667.9 81.1 %all-gather.26.cloned.1.call-done = bf16[2,1024,1408]{1,2,0:T(8,128)(2,1)} async-done(((bf16[2,256,1408]{1,2,0:T(8,128)(2,1)}), bf16[2,1024,1408]{1,2,0:T(8,128)(2,1)}) %all-gather.26.cloned.1.call-update) | async-done | bytes 5767184 | tf_op jit(solution)/shard_map/all_gather | solution.py:310
  749.0 106.0 %all-gather.28.cloned.1.call-done = bf16[2,1024,1408]{1,2,0:T(8,128)(2,1)} async-done(((bf16[2,256,1408]{1,2,0:T(8,128)(2,1)}), bf16[2,1024,1408]{1,2,0:T(8,128)(2,1)}) %all-gather.28.cloned.1.call-update) | async-done | bytes 5767184 | tf_op jit(solution)/shard_map/all_gather | solution.py:309
  976.7 85.6 %all-gather.40.cloned.1.call-done = bf16[1408,6144]{1,0:T(8,128)(2,1)} async-done(((bf16[176,6144]{1,0:T(8,128)(2,1)}), bf16[1408,6144]{1,0:T(8,128)(2,1)}) %all-gather.40.cloned.1.call-update) | async-done | bytes 17301520 | tf_op jit(solution)/shard_map/all_gather | solution.py:186
  1079.6 76.7 %all-gather.44.cloned.1.call-done = bf16[6144,1408]{1,0:T(8,128)(2,1)} async-done(((bf16[768,1408]{1,0:T(8,128)(2,1)}), bf16[6144,1408]{1,0:T(8,128)(2,1)}) %all-gather.44.cloned.1.call-update) | async-done | bytes 17301520 | tf_op jit(solution)/shard_map/all_gather | solution.py:187
  1220.2 42.3 %while.66 = (s32[]{:T(128)}, f32[2,256,16,88]{1,3,2,0:T(8,128)}, f32[2,333,16,88]{1,3,2,0:T(8,128)}, f32[2,333,16,88]{1,3,2,0:T(8,128)}, bf16[2,333,16,88]{1,3,2...) while((s32[]{:T(128)}, f32[2,256,16,88]{1,3,2,0:T(8,128)}, ...), condition=%wide.region_29.30_spmd, body=%wide.region_27.0_spmd.sunk | while | flops 606281728 | bytes 32285908 | solution.py:162
  1295.4 65.6 %while.67 = (s32[]{:T(128)}, f32[2,256,16,88]{1,3,2,0:T(8,128)}, bf16[2,1024,16,88]{1,3,2,0:T(8,128)(2,1)}, bf16[2,1024,16,88]{1,3,2,0:T(8,128)(2,1)}, bf16[2,10...) while((s32[]{:T(128)}, f32[2,256,16,88]{1,3,2,0:T(8,128)}, ...), condition=%wide.region_36.37_spmd, body=%wide.region_34.0_spmd.sunk | while | flops 1864366080 | bytes 115602696 | solution.py:162
  1421.5 42.0 %reduce-scatter.36.cloned.1.call-done = bf16[2,256,1408]{1,2,0:T(8,128)(2,1)} async-done(((bf16[2,1024,1408]{1,2,0:T(8,128)(2,1)}), bf16[2,256,1408]{1,2,0:T(8,128)(2,1)}) %reduce-scatter.36.cloned.1.call-update) | async-done | bytes 1441808 | tf_op jit(solution)/shard_map/reduce_scatter | solution.py:383
  1481.6 87.0 %reduce-scatter.34.cloned.1.call-done = bf16[2,256,1408]{1,2,0:T(8,128)(2,1)} async-done(((bf16[2,1024,1408]{1,2,0:T(8,128)(2,1)}), bf16[2,256,1408]{1,2,0:T(8,128)(2,1)}) %reduce-scatter.34.cloned.1.call-update) | async-done | bytes 1441808 | tf_op jit(solution)/shard_map/reduce_scatter | solution.py:389
  1736.0 49.6 %reduce-scatter.44.cloned.1.call-done = f32[176,1408]{1,0:T(8,128)} async-done(((f32[1408,1408]{1,0:T(8,128)}), f32[176,1408]{1,0:T(8,128)}) %reduce-scatter.44.cloned.1.call-update) | async-done | bytes 991248 | tf_op jit(solution)/shard_map/reduce_scatter | solution.py:231
  1788.1 70.0 %reduce-scatter.46.cloned.1.call-done = f32[176,1408]{1,0:T(8,128)} async-done(((f32[1408,1408]{1,0:T(8,128)}), f32[176,1408]{1,0:T(8,128)}) %reduce-scatter.46.cloned.1.call-update) | async-done | bytes 991248 | tf_op jit(solution)/shard_map/reduce_scatter | solution.py:232
  1860.6 70.6 %reduce-scatter.50.cloned.1.call-done = f32[176,1408]{1,0:T(8,128)} async-done(((f32[1408,1408]{1,0:T(8,128)}), f32[176,1408]{1,0:T(8,128)}) %reduce-scatter.50.cloned.1.call-update) | async-done | bytes 991248 | tf_op jit(solution)/shard_map/reduce_scatter | solution.py:233
  1933.7 70.2 %reduce-scatter.40.cloned.1.call-done = f32[176,1408]{1,0:T(8,128)} async-done(((f32[1408,1408]{1,0:T(8,128)}), f32[176,1408]{1,0:T(8,128)}) %reduce-scatter.40.cloned.1.call-update) | async-done | bytes 991248 | tf_op jit(solution)/shard_map/reduce_scatter | solution.py:229
  2006.4 113.4 %reduce-scatter.38.cloned.1.call-done = f32[352,1408]{1,0:T(8,128)} async-done(((f32[2816,1408]{1,0:T(8,128)}), f32[352,1408]{1,0:T(8,128)}) %reduce-scatter.38.cloned.1.call-update) | async-done | bytes 1982480 | tf_op jit(solution)/shard_map/reduce_scatter | solution.py:228
  2124.8 149.4 %reduce-scatter.42.cloned.1.call-done = f32[176,4224]{1,0:T(8,128)} async-done(((f32[1408,4224]{1,0:T(8,128)}), f32[176,4224]{1,0:T(8,128)}) %reduce-scatter.42.cloned.1.call-update) | async-done | bytes 2973712 | tf_op jit(solution)/shard_map/reduce_scatter | solution.py:230
  2281.2 207.6 %reduce-scatter.56.cloned.1.call-done = f32[768,1408]{1,0:T(8,128)} async-done(((f32[6144,1408]{1,0:T(8,128)}), f32[768,1408]{1,0:T(8,128)}) %reduce-scatter.56.cloned.1.call-update) | async-done | bytes 4325392 | tf_op jit(solution)/shard_map/reduce_scatter | solution.py:235
  2496.9 206.4 %reduce-scatter.52.cloned.1.call-done = f32[176,6144]{1,0:T(8,128)} async-done(((f32[1408,6144]{1,0:T(8,128)}), f32[176,6144]{1,0:T(8,128)}) %reduce-scatter.52.cloned.1.call-update) | async-done | bytes 4325392 | tf_op jit(solution)/shard_map/reduce_scatter | solution.py:234
  2742.9 125.6 %all-reduce.14.cloned.1.call-done = (f32[2816]{0:T(1024)}, f32[2816]{0:T(1024)}, f32[1408]{0:T(1024)}, f32[1408]{0:T(1024)}, f32[1408]{0:T(1024)}, /*index=5*/f3...) async-done(((f32[2816]{0:T(1024)}, f32[2816]{0:T(1024)}, ...) | async-done | bytes 139696 | tf_op jit(solution)/shard_map/psum | solution.py:430
  3000.2 43.9 %reduce-scatter.62.cloned.1.call-done = bf16[1056,176]{1,0:T(8,128)(2,1)} async-done(((bf16[4224,176]{1,0:T(8,128)(2,1)}), bf16[1056,176]{1,0:T(8,128)(2,1)}) %reduce-scatter.62.cloned.1.call-update) | async-done | bytes 371728
  3046.6 44.2 %reduce-scatter.70.cloned.1.call-done = bf16[352,768]{1,0:T(8,128)(2,1)} async-done(((bf16[1408,768]{1,0:T(8,128)(2,1)}), bf16[352,768]{1,0:T(8,128)(2,1)}) %reduce-scatter.70.cloned.1.call-update) | async-done | bytes 540688
  3093.4 44.2 %reduce-scatter.54.cloned.1.call-done = bf16[176,1536]{1,0:T(8,128)(2,1)} async-done(((bf16[176,6144]{1,0:T(8,128)(2,1)}), bf16[176,1536]{1,0:T(8,128)(2,1)}) %reduce-scatter.54.cloned.1.call-update) | async-done | bytes 540688 | tf_op jit(solution)/shard_map/reduce_scatter | solution.py:217
  3139.7 46.0 %reduce-scatter.48.cloned.1.call-done = f32[352,256]{1,0:T(8,128)} async-done(((f32[2816,256]{1,0:T(8,128)}), f32[352,256]{1,0:T(8,128)}) %reduce-scatter.48.cloned.1.call-update) | async-done | bytes 360464 | tf_op jit(solution)/shard_map/reduce_scatter | solution.py:236
  (805 shorter events, 1144.8 us)
Async XLA Ops:
  76.9 565.3 %all-reduce.10.cloned.1.call-start = ((), (), s32[]{:S(2)}) async-start(), calls=%async_computation.26 | async-start | bytes 15138816 | tf_op jit(solution)/shard_map/psum | solution.py:325
  101.2 647.8 %all-gather.26.cloned.1.call-start = ((), (), s32[]{:S(2)}) async-start(), calls=%async_computation.22 | async-start | bytes 7208960 | tf_op jit(solution)/shard_map/all_gather | solution.py:310
  285.6 569.4 %all-gather.28.cloned.1.call-start = ((), (), s32[]{:S(2)}) async-start(), calls=%async_computation.23 | async-start | bytes 7208960 | tf_op jit(solution)/shard_map/all_gather | solution.py:309
  300.5 591.1 %all-gather.30.cloned.1.call-start = ((), (), s32[]{:S(2)}) async-start(), calls=%async_computation.24 | async-start | bytes 4460544 | tf_op jit(solution)/shard_map/all_gather | solution.py:183
  320.5 609.4 %all-gather.34.cloned.1.call-start = ((), (), s32[]{:S(2)}) async-start(), calls=%async_computation.27 | async-start | bytes 4460544 | tf_op jit(solution)/shard_map/all_gather | solution.py:184
  343.0 625.2 %all-gather.36.cloned.1.call-start = ((), (), s32[]{:S(2)}) async-start(), calls=%async_computation.28 | async-start | bytes 4460544 | tf_op jit(solution)/shard_map/all_gather | solution.py:185
  366.9 695.4 %all-gather.40.cloned.1.call-start = ((), (), s32[]{:S(2)}) async-start(), calls=%async_computation.30 | async-start | bytes 19464192 | tf_op jit(solution)/shard_map/all_gather | solution.py:186
  367.5 788.8 %all-gather.44.cloned.1.call-start = ((), (), s32[]{:S(2)}) async-start(), calls=%async_computation.32 | async-start | bytes 19464192 | tf_op jit(solution)/shard_map/all_gather | solution.py:187
  379.9 1083.6 %reduce-scatter.36.cloned.1.call-start = ((), (), s32[]{:S(2)}) async-start(), calls=%async_computation.34 | async-start | bytes 7208960 | tf_op jit(solution)/shard_map/reduce_scatter | solution.py:383
  1410.5 520.8 %reduce-scatter.50.cloned.1.call-start = ((), (), s32[]{:S(2)}) async-start(), calls=%async_computation.42 | async-start | bytes 8921088 | tf_op jit(solution)/shard_map/reduce_scatter | solution.py:233
  1417.8 586.1 %reduce-scatter.40.cloned.1.call-start = ((), (), s32[]{:S(2)}) async-start(), calls=%async_computation.37 | async-start | bytes 8921088 | tf_op jit(solution)/shard_map/reduce_scatter | solution.py:229
  1594.0 525.8 %reduce-scatter.38.cloned.1.call-start = ((), (), s32[]{:S(2)}) async-start(), calls=%async_computation.36 | async-start | bytes 17842176 | tf_op jit(solution)/shard_map/reduce_scatter | solution.py:228
  1608.8 665.4 %reduce-scatter.42.cloned.1.call-start = ((), (), s32[]{:S(2)}) async-start(), calls=%async_computation.38 | async-start | bytes 26763264 | tf_op jit(solution)/shard_map/reduce_scatter | solution.py:230
  1623.7 865.0 %reduce-scatter.56.cloned.1.call-start = ((), (), s32[]{:S(2)}) async-start(), calls=%async_computation.45 | async-start | bytes 38928384 | tf_op jit(solution)/shard_map/reduce_scatter | solution.py:235
  1650.3 1053.0 %reduce-scatter.52.cloned.1.call-start = ((), (), s32[]{:S(2)}) async-start(), calls=%async_computation.43 | async-start | bytes 38928384 | tf_op jit(solution)/shard_map/reduce_scatter | solution.py:234
  1670.4 1198.1 %all-reduce.14.cloned.1.call-start = ((), (), s32[]{:S(2)}) async-start(), calls=%async_computation.54 | async-start | bytes 351232 | tf_op jit(solution)/shard_map/psum | solution.py:430
  1735.9 1159.7 %reduce-scatter.64.cloned.1.call-start = ((), (), s32[]{:S(2)}) async-start(), calls=%async_computation.50 | async-start | bytes 901120
  1788.0 1131.8 %reduce-scatter.66.cloned.1.call-start = ((), (), s32[]{:S(2)}) async-start(), calls=%async_computation.51 | async-start | bytes 901120
  1860.5 1083.3 %reduce-scatter.68.cloned.1.call-start = ((), (), s32[]{:S(2)}) async-start(), calls=%async_computation.52 | async-start | bytes 901120
  1933.6 1034.9 %reduce-scatter.60.cloned.1.call-start = ((), (), s32[]{:S(2)}) async-start(), calls=%async_computation.48 | async-start | bytes 901120
  2006.4 991.9 %reduce-scatter.58.cloned.1.call-start = ((), (), s32[]{:S(2)}) async-start(), calls=%async_computation.47 | async-start | bytes 1351680
  2124.8 919.4 %reduce-scatter.62.cloned.1.call-start = ((), (), s32[]{:S(2)}) async-start(), calls=%async_computation.49 | async-start | bytes 2703360
  2281.1 809.7 %reduce-scatter.70.cloned.1.call-start = ((), (), s32[]{:S(2)}) async-start(), calls=%async_computation.53 | async-start | bytes 2703360
  2496.8 640.7 %reduce-scatter.54.cloned.1.call-start = ((), (), s32[]{:S(2)}) async-start(), calls=%async_computation.44 | async-start | bytes 2703360 | tf_op jit(solution)/shard_map/reduce_scatter | solution.py:217
  (213 other events, 11554.4 us)
Sparse Core Ops, SparseCore 0:
  9.6 59.4 all-gather.45
  136.3 52.4 all-gather.19
  191.1 69.2 all-gather.23
  261.8 50.3 all-gather.37
  313.8 61.9 all-gather.41
  378.1 264.0 all-reduce.9
  643.8 105.1 all-gather.25
  750.5 104.4 all-gather.27
  970.2 92.0 all-gather.39
  1064.2 92.0 all-gather.43
  1361.2 102.2 reduce-scatter.35
  1465.8 102.7 reduce-scatter.33
  1570.9 142.4 all-reduce.11
  1717.4 68.0 reduce-scatter.43
  1789.0 69.0 reduce-scatter.45
  1862.1 69.0 reduce-scatter.49
  1934.8 69.0 reduce-scatter.39
  2008.1 111.6 reduce-scatter.37
  2123.3 150.8 reduce-scatter.41
  2278.2 210.4 reduce-scatter.55
  2492.7 210.4 reduce-scatter.51
  2713.5 154.9 all-reduce.13
  3046.5 44.2 reduce-scatter.69
  3093.2 44.2 reduce-scatter.53
  (12 shorter events, 369.5 us)
where the time goes:
time: 3210 us
  waiting for transfers between devices  2360 us (74%)
  matrix products  395 us (12%)
  other arithmetic  155 us (5%)
  local copies, waits for them, and re-layouts  153 us (5%)
  blocking collectives  121 us (4%)
    psum x1, waiting for transfers between devices, body(): text_kv = lax.psum(text_part, 'fsdp') + kv2_b  262 us
    unnamed x43, waiting for transfers between devices  215 us
    reduce_scatter x1, waiting for transfers between devices, reduce_rows(): lax.psum_scatter(gradients[7], 'dp', scatter_dimension=0, tiled=True)  208 us
    reduce_scatter x1, waiting for transfers between devices, reduce_rows(): lax.psum_scatter(gradients[6], 'dp', scatter_dimension=0, tiled=True)  206 us
    reduce_scatter x1, waiting for transfers between devices, reduce_rows(): lax.psum_scatter(gradients[2], 'dp', scatter_dimension=0, tiled=True)  149 us
    psum x1, waiting for transfers between devices, body(): lax.psum((gain_skip, bias_skip_norm, bias_skip, bias_ada, gain_n1, bias_n...  126 us
    reduce_scatter x1, waiting for transfers between devices, reduce_rows(): lax.psum_scatter(gradients[0], 'dp', scatter_dimension=0, tiled=True)  113 us
    all_gather x1, waiting for transfers between devices, body(): lax.all_gather(key_low, 'fsdp', axis=1, tiled=True)  106 us
  transfers between devices with their start and end apart: 36, of which 34 were waited for; matrix products, arithmetic and copies ran while one was open for 14% of the time, Pallas kernels for 0%

commit v1 on v0

v1 whole, which is shorter than its diff:
```python
from functools import partial
import math

import jax
import jax.numpy as jnp
from jax import lax
from jax.experimental import pallas as pl
from jax.experimental.pallas import tpu as pltpu
from jax.sharding import PartitionSpec as P

norm_eps = 1e-06


def layer_norm(values, norm_gain, norm_bias):
    center = values - jnp.mean(values, axis=-1, keepdims=True)
    spread = jnp.mean(center * center, axis=-1, keepdims=True)
    return center * lax.rsqrt(spread + norm_eps) * norm_gain + norm_bias


def time_embedding(timestep, model_width):
    halfway = model_width // 2
    frequency = jnp.exp(jnp.arange(halfway, dtype=jnp.float32) * (-math.log(10000.0) / halfway))
    angles = timestep.astype(jnp.float32)[:, None] * frequency
    return jnp.concatenate([jnp.cos(angles), jnp.sin(angles)], axis=-1)


def text_heads(text_kv, knorm_gain):
    heads = text_kv.reshape(-1, knorm_gain.shape[0], text_kv.shape[1])
    key_heads, value_heads = jnp.split(heads, 2)
    center = key_heads - jnp.mean(key_heads, axis=1, keepdims=True)
    spread = jnp.mean(center * center, axis=1, keepdims=True)
    key_heads = center * lax.rsqrt(spread + norm_eps) * knorm_gain[None, :, None]
    return jnp.concatenate([key_heads, value_heads])


def gelu_tanh(pre_values):
    return jax.nn.gelu(pre_values, approximate=True)


def project(inputs, weight):
    return jnp.dot(inputs, weight, preferred_element_type=jnp.float32)


def project_back(grad_low, weight):
    return lax.dot_general(
        grad_low,
        weight,
        (((grad_low.ndim - 1,), (1,)), ((), ())),
        preferred_element_type=jnp.float32,
    )


def project_sublanes(inputs_turned, weight):
    return lax.dot_general(
        inputs_turned, weight, (((0,), (0,)), ((), ())), preferred_element_type=jnp.float32
    )


def project_turned(inputs, weight):
    return lax.dot_general(
        weight, inputs, (((0,), (1,)), ((), ())), preferred_element_type=jnp.float32
    )


def project_back_turned(grad_low, weight):
    return lax.dot_general(
        weight, grad_low, (((1,), (1,)), ((), ())), preferred_element_type=jnp.float32
    )


def column_sum(grad_low):
    return jnp.sum(grad_low.reshape(-1, grad_low.shape[-1]), axis=0, dtype=jnp.float32)


def lane_dot(left, right):
    return lax.dot_general(
        left, right, (((1,), (1,)), ((), ())), preferred_element_type=jnp.float32
    )


def row_dot(left, right):
    return lax.dot_general(
        left, right, (((0,), (0,)), ((), ())), preferred_element_type=jnp.float32
    )


def swap_quarters(values):
    quarter = values.shape[0] // 4
    pieces = [values[index * quarter : (index + 1) * quarter] for index in (1, 0, 3, 2)]
    return jnp.concatenate(pieces, axis=0)


def turn_tables(position_grid, head_size):
    quarter = head_size // 4
    frequency = jnp.exp(jnp.arange(quarter, dtype=jnp.float32) * (-math.log(10000.0) / quarter))
    row_angle = frequency[:, None] * position_grid[0].astype(jnp.float32)
    col_angle = frequency[:, None] * position_grid[1].astype(jnp.float32)
    row_sin, col_sin = jnp.sin(row_angle), jnp.sin(col_angle)
    row_cos, col_cos = jnp.cos(row_angle), jnp.cos(col_angle)
    return (
        jnp.concatenate([row_cos, row_cos, col_cos, col_cos]),
        jnp.concatenate([-row_sin, row_sin, -col_sin, col_sin]),
    )


def normalize(values):
    center = values - jnp.mean(values, axis=0, keepdims=True)
    spread = lax.rsqrt(jnp.mean(center * center, axis=0, keepdims=True) + norm_eps)
    return (center * spread, spread)


def turn_kernel(normed_parts, gain_ref, bias_ref, cos_ref, sin_ref, in_ref, out_ref):
    part = pl.program_id(0)

    @pl.when(part < normed_parts)
    def _():
        scaled = normalize(in_ref[0])[0] * gain_ref[0] + bias_ref[0]
        turned = scaled * cos_ref[...] + swap_quarters(scaled) * sin_ref[...]
        factor = jnp.where(part == 0, in_ref.shape[1] ** (-0.5), 1.0)
        out_ref[0] = (turned * factor).astype(out_ref.dtype)

    @pl.when(part >= normed_parts)
    def _():
        out_ref[0] = in_ref[0].astype(out_ref.dtype)


def turn_heads(heads, gains, biases, tables, head_count):
    count, head_size, tokens = heads.shape
    normed_parts = gains.shape[0]
    last = normed_parts - 1
    vector = pl.BlockSpec((1, head_size, 1), lambda part, head: (jnp.minimum(part, last), 0, 0))
    table = pl.BlockSpec((head_size, tokens), lambda part, head: (0, 0))
    block = pl.BlockSpec(
        (1, head_size, tokens), lambda part, head: (part * head_count + head, 0, 0)
    )
    return pl.pallas_call(
        partial(turn_kernel, normed_parts),
        grid=(count // head_count, head_count),
        in_specs=[vector, vector, table, table, block],
        out_specs=block,
        out_shape=jax.ShapeDtypeStruct(heads.shape, jnp.bfloat16),
        compiler_params=pltpu.CompilerParams(vmem_limit_bytes=24 * 2**20),
        cost_estimate=pl.CostEstimate(
            flops=20 * heads.size, bytes_accessed=6 * heads.size, transcendentals=0
        ),
    )(gains[:, :, None], biases[:, :, None], *tables, heads)


def turn_back_kernel(
    normed_parts, gain_ref, cos_ref, sin_ref, in_ref, grad_ref, *refs
):
    part, head = pl.program_id(0), pl.program_id(1)
    out_ref, gain_out, bias_out = refs[-3:]
    gradient = grad_ref[0]
    if len(refs) > 3:
        held = refs[0][0] + refs[1][0].astype(jnp.float32)
        gradient = jnp.where(part == 0, gradient, held)

    @pl.when(part < normed_parts)
    def _():
        factor = jnp.where(part == 0, in_ref.shape[1] ** (-0.5), 1.0)
        scaled = gradient * factor
        back = scaled * cos_ref[...] + swap_quarters(scaled * sin_ref[...])
        hat, spread = normalize(in_ref[0])
        gain_term = back * hat

        @pl.when(head == 0)
        def _():
            gain_out[0] = gain_term
            bias_out[0] = back

        @pl.when(head > 0)
        def _():
            gain_out[0] += gain_term
            bias_out[0] += back

        grad_hat = back * gain_ref[0]
        center = grad_hat - jnp.mean(grad_hat, axis=0, keepdims=True)
        along = jnp.mean(grad_hat * hat, axis=0, keepdims=True)
        out_ref[0] = spread * (center - hat * along)

    @pl.when(part >= normed_parts)
    def _():
        out_ref[0] = gradient


def turn_heads_back(heads, query_grads, kv_grads, gains, tables, head_count):
    count, head_size, tokens = heads.shape
    normed_parts = gains.shape[0]
    last = normed_parts - 1
    shape = (1, head_size, tokens)
    vector = pl.BlockSpec((1, head_size, 1), lambda part, head: (jnp.minimum(part, last), 0, 0))
    table = pl.BlockSpec((head_size, tokens), lambda part, head: (0, 0))
    block = pl.BlockSpec(shape, lambda part, head: (part * head_count + head, 0, 0))
    first = pl.BlockSpec(
        shape, lambda part, head: (jnp.where(part == 0, head, head_count - 1), 0, 0)
    )
    later = pl.BlockSpec(
        shape,
        lambda part, head: (jnp.where(part == 0, 0, (part - 1) * head_count + head), 0, 0),
    )
    total = pl.BlockSpec(shape, lambda part, head: (jnp.minimum(part, last), 0, 0))
    in_specs = [vector, table, table, block, first] + [later] * len(kv_grads)
    operands = [gains[:, :, None], *tables, heads, query_grads, *kv_grads]
    kernel = partial(turn_back_kernel, normed_parts)
    totals = jax.ShapeDtypeStruct((normed_parts, head_size, tokens), jnp.float32)
    out, gain_sum, bias_sum = pl.pallas_call(
        kernel,
        grid=(count // head_count, head_count),
        in_specs=in_specs,
        out_specs=[block, total, total],
        out_shape=[jax.ShapeDtypeStruct(heads.shape, jnp.float32), totals, totals],
        compiler_params=pltpu.CompilerParams(vmem_limit_bytes=24 * 2**20),
        cost_estimate=pl.CostEstimate(
            flops=40 * heads.size, bytes_accessed=12 * heads.size, transcendentals=0
        ),
    )(*operands)
    return (out, jnp.sum(gain_sum, axis=-1), jnp.sum(bias_sum, axis=-1))


def joined_rows(refs):
    if len(refs) == 1:
        return refs[0][0]
    return jnp.concatenate([ref[0] for ref in refs], axis=-1)


def attend_kernel(key_count, piece_count, query_ref, *refs):
    keys = joined_rows(refs[:piece_count])
    values = joined_rows(refs[piece_count : 2 * piece_count])
    out_ref, log_ref = refs[2 * piece_count :]
    weights = jnp.exp(row_dot(keys, query_ref[0]))
    if key_count < keys.shape[1]:
        row = lax.broadcasted_iota(jnp.int32, weights.shape, 0)
        weights = jnp.where(row < key_count, weights, 0.0)
    total = jnp.sum(weights, axis=0, keepdims=True)
    mixed = jnp.dot(values, weights.astype(jnp.bfloat16), preferred_element_type=jnp.float32)
    out_ref[0] = mixed / total
    log_ref[0] = jnp.log(total)


def head_block(array, offset):
    return pl.BlockSpec((1,) + array.shape[1:], lambda head: (head + offset, 0, 0))


def attend_cost(head_count, head_size, tokens, keys, products):
    return pl.CostEstimate(
        flops=2 * products * head_count * head_size * tokens * keys,
        bytes_accessed=8 * head_count * head_size * (tokens + keys),
        transcendentals=head_count * tokens * keys,
    )


def attend(queries, pieces, key_count):
    head_count = pieces[0].shape[0] // 2
    head_size, tokens = queries.shape[1:]
    keys = sum(piece.shape[2] for piece in pieces)
    return pl.pallas_call(
        partial(attend_kernel, key_count, len(pieces)),
        grid=(head_count,),
        in_specs=[head_block(queries, 0)]
        + [head_block(piece, 0) for piece in pieces]
        + [head_block(piece, head_count) for piece in pieces],
        out_specs=[
            pl.BlockSpec((1, head_size, tokens), lambda head: (head, 0, 0)),
            pl.BlockSpec((1, 1, tokens), lambda head: (head, 0, 0)),
        ],
        out_shape=[
            jax.ShapeDtypeStruct((head_count, head_size, tokens), jnp.float32),
            jax.ShapeDtypeStruct((head_count, 1, tokens), jnp.float32),
        ],
        compiler_params=pltpu.CompilerParams(vmem_limit_bytes=32 * 2**20),
        cost_estimate=attend_cost(head_count, head_size, tokens, keys, 2),
    )(queries, *pieces, *pieces)


def attend_back_kernel(key_count, piece_count, query_ref, grad_ref, mixed_ref, log_ref, *refs):
    keys = joined_rows(refs[:piece_count])
    values = joined_rows(refs[piece_count : 2 * piece_count])
    outs = refs[2 * piece_count :]
    queries = query_ref[0]
    gradient = grad_ref[0]
    grad_low = gradient.astype(jnp.bfloat16)
    probs = jnp.exp(row_dot(keys, queries) - log_ref[0])
    if key_count < keys.shape[1]:
        row = lax.broadcasted_iota(jnp.int32, probs.shape, 0)
        probs = jnp.where(row < key_count, probs, 0.0)
    along = jnp.sum(grad_low.astype(jnp.float32) * mixed_ref[0], axis=0, keepdims=True)
    grad_scores = (probs * (row_dot(values, grad_low) - along)).astype(jnp.bfloat16)
    outs[0][0] = jnp.dot(keys, grad_scores, preferred_element_type=jnp.float32)
    grad_keys = lane_dot(queries, grad_scores)
    grad_values = lane_dot(grad_low, probs.astype(jnp.bfloat16))
    start = 0
    for index in range(piece_count):
        stop = start + refs[index].shape[2]
        outs[1 + index][0, 0] = grad_keys[:, start:stop].astype(outs[1 + index].dtype)
        outs[1 + index][1, 0] = grad_values[:, start:stop].astype(outs[1 + index].dtype)
        start = stop


def attend_back(queries, gradient, mixed, log_total, pieces, key_count, kinds):
    head_count = pieces[0].shape[0] // 2
    head_size, tokens = queries.shape[1:]
    keys = sum(piece.shape[2] for piece in pieces)
    return pl.pallas_call(
        partial(attend_back_kernel, key_count, len(pieces)),
        grid=(head_count,),
        in_specs=[head_block(array, 0) for array in (queries, gradient, mixed, log_total)]
        + [head_block(piece, 0) for piece in pieces]
        + [head_block(piece, head_count) for piece in pieces],
        out_specs=[pl.BlockSpec((1, head_size, tokens), lambda head: (head, 0, 0))]
        + [
            pl.BlockSpec((2, 1) + piece.shape[1:], lambda head: (0, head, 0, 0)) for piece in pieces
        ],
        out_shape=[jax.ShapeDtypeStruct((head_count, head_size, tokens), jnp.float32)]
        + [
            jax.ShapeDtypeStruct((2, head_count) + piece.shape[1:], kind)
            for piece, kind in zip(pieces, kinds)
        ],
        compiler_params=pltpu.CompilerParams(vmem_limit_bytes=40 * 2**20),
        cost_estimate=attend_cost(head_count, head_size, tokens, keys, 5),
    )(queries, gradient, mixed, log_total, *pieces, *pieces)


def swap_pairs(size, bit):
    return [(index, index ^ bit) for index in range(size)]


def token_routes(dp_size, fsdp_size, flip):
    route = []
    for position in range(dp_size * fsdp_size):
        row, column = divmod(position, fsdp_size)
        core = row % 2
        target_row = row - core + column // 2
        route.append((position, target_row * fsdp_size + 2 * core + (column + flip) % 2))
    return route


def trade(pair, dp_size, fsdp_size):
    return tuple(
        lax.ppermute(part, ("dp", "fsdp"), token_routes(dp_size, fsdp_size, flip))
        for flip, part in enumerate(pair)
    )


def ordered(is_odd, first, second):
    return (jnp.where(is_odd, second, first), jnp.where(is_odd, first, second))


def trade_in(values, is_odd, sizes):
    return trade(ordered(is_odd, values[0], values[1]), *sizes)


def trade_out(first, second, is_odd, sizes):
    return jnp.stack(ordered(is_odd, *trade((first, second), *sizes)))


def column_gather(shard, place, fsdp_size):
    other = lax.ppermute(shard, "fsdp", swap_pairs(fsdp_size, 2))
    held = jnp.stack(ordered(place // 2 == 1, shard, other))
    other = lax.ppermute(held, "fsdp", swap_pairs(fsdp_size, 1))
    even, odd = ordered(place % 2 == 1, held, other)
    return jnp.concatenate([even[0], odd[0], even[1], odd[1]], axis=-1)


def column_scatter(grad_rows, place, fsdp_size):
    blocks = jnp.split(grad_rows, fsdp_size, axis=-1)
    even = jnp.stack([blocks[0], blocks[2]])
    odd = jnp.stack([blocks[1], blocks[3]])
    own, given = ordered(place % 2 == 1, even, odd)
    taken = lax.ppermute(given, "fsdp", swap_pairs(fsdp_size, 1))
    summed = own.astype(jnp.float32) + taken.astype(jnp.float32)
    own, given = ordered(place // 2 == 1, summed[0], summed[1])
    taken = lax.ppermute(given.astype(jnp.bfloat16), "fsdp", swap_pairs(fsdp_size, 2))
    return own + taken.astype(jnp.float32)


def row_gather(rows):
    return lax.all_gather(rows, "dp", axis=0, tiled=True)


def row_scatter(gradient):
    return lax.psum_scatter(gradient, "dp", scatter_dimension=0, tiled=True)


def butterfly_gather(values, axis_name, size, index):
    step = 1
    while step < size:
        other = lax.ppermute(values, axis_name, swap_pairs(size, step))
        values = jnp.concatenate(ordered((index // step) % 2 == 1, values, other), axis=0)
        step *= 2
    return values


def butterfly_sum(values, axis_name, size):
    step = 1
    while step < size:
        values = values + lax.ppermute(values, axis_name, swap_pairs(size, step))
        step *= 2
    return values


def pack_rows(vectors, width):
    rows = []
    for vector in vectors:
        count = -(-vector.shape[0] // width)
        rows.append(jnp.pad(vector, (0, count * width - vector.shape[0])).reshape(count, width))
    return jnp.concatenate(rows)


def unpack_rows(packed, vectors):
    parts = []
    start = 0
    for vector in vectors:
        count = -(-vector.shape[0] // packed.shape[1])
        parts.append(packed[start : start + count].reshape(-1)[: vector.shape[0]])
        start += count
    return parts


def after(values, *earlier):
    corner = (slice(0, 1),) * values.ndim
    wait = sum(
        part[(slice(0, 1),) * part.ndim].reshape((1,) * values.ndim).astype(jnp.float32)
        for part in earlier
    )
    return values.at[corner].set(values[corner] + (wait * 0).astype(values.dtype))


def low_rows(inputs_turned, grad_low):
    return jnp.dot(inputs_turned, grad_low, preferred_element_type=jnp.float32).astype(jnp.bfloat16)


def low_lanes(inputs, grad_turned):
    return lax.dot_general(
        inputs, grad_turned, (((0,), (1,)), ((), ())), preferred_element_type=jnp.float32
    ).astype(jnp.bfloat16)


def back_sublanes(grad_turned, weight):
    return lax.dot_general(
        grad_turned, weight, (((0,), (1,)), ((), ())), preferred_element_type=jnp.float32
    )


def low_grad(inputs, grad_low):
    return lax.dot_general(
        inputs, grad_low, (((0,), (0,)), ((), ())), preferred_element_type=jnp.float32
    ).astype(jnp.bfloat16)


def body(
    dp_size,
    fsdp_size,
    latent,
    skip_state,
    text_states,
    timestep,
    position_grid,
    cotangent,
    skip_gain,
    skip_bias,
    skip_w,
    skip_b,
    ada_w,
    ada_b,
    norm1_gain,
    norm1_bias,
    qkv_w,
    qkv_b,
    qnorm1_gain,
    qnorm1_bias,
    knorm1_gain,
    knorm1_bias,
    proj1_w,
    proj1_b,
    norm3_gain,
    norm3_bias,
    q2_w,
    q2_b,
    kv2_w,
    kv2_b,
    qnorm2_gain,
    qnorm2_bias,
    knorm2_gain,
    proj2_w,
    proj2_b,
    norm2_gain,
    norm2_bias,
    fc1_w,
    fc1_b,
    fc2_w,
    fc2_b,
):
    model_width = latent.shape[-1]
    head_size = qnorm1_gain.shape[0]
    head_count = model_width // head_size
    sizes = (dp_size, fsdp_size)
    place = lax.axis_index("fsdp")
    row_place = lax.axis_index("dp")
    core = row_place % 2
    is_odd = place % 2 == 1
    columns = partial(column_gather, place=place, fsdp_size=fsdp_size)

    pair = swap_pairs(dp_size, 1)
    w_skip = row_gather(columns(skip_w))
    qkv_rows = columns(qkv_w)
    w_qkv = row_gather(after(qkv_rows, w_skip))
    kv2_rows = columns(kv2_w)
    w_kv2 = row_gather(after(kv2_rows, w_qkv))
    square_rows = columns(jnp.concatenate([proj1_w, q2_w, proj2_w]))
    square_rows = square_rows.reshape(3, -1, model_width)
    both_in = jnp.concatenate([latent, skip_state], axis=-1)
    both_in = after(both_in, kv2_rows, square_rows)
    both_in = jnp.concatenate(trade_in(both_in, is_odd, sizes))
    grid_in = jnp.concatenate(trade_in(position_grid, is_odd, sizes), axis=-1)
    tables = turn_tables(grid_in, head_size)

    times = butterfly_gather(timestep, "dp", dp_size, row_place)
    embed_act = jax.nn.silu(time_embedding(times, model_width)).astype(jnp.bfloat16)
    ada_rows = ada_w.shape[0]
    embed_own = lax.dynamic_slice_in_dim(embed_act, row_place * ada_rows, ada_rows, 1)
    shift_part = butterfly_sum(project(embed_own, ada_w), "dp", dp_size)
    own_rows = lax.dynamic_slice_in_dim(shift_part, (row_place // 2) * 4, 4, 0)
    shift_rows = columns(own_rows) + ada_b
    shift = lax.dynamic_slice_in_dim(shift_rows, place, 1, 0)

    joined_in = both_in.astype(jnp.float32)
    joined = layer_norm(joined_in, skip_gain, skip_bias).astype(jnp.bfloat16)
    resid_one = project(joined, w_skip) + skip_b
    squares = lax.all_gather(after(square_rows, w_kv2, joined), "dp", axis=1, tiled=True)
    w_proj1, w_q2, w_proj2 = squares
    normed = (layer_norm(resid_one, norm1_gain, norm1_bias) + shift).astype(jnp.bfloat16)
    qkv_turned = project_turned(normed, w_qkv) + qkv_b[:, None]
    qkv_heads = qkv_turned.reshape(3 * head_count, head_size, -1)
    self_gains = jnp.stack([qnorm1_gain, knorm1_gain])
    self_biases = jnp.stack([qnorm1_bias, knorm1_bias])
    heads_low = turn_heads(qkv_heads, self_gains, self_biases, tables, head_count)
    kv_own = heads_low[head_count:]
    kv_other = lax.ppermute(kv_own, "dp", pair)
    mixed, self_log = attend(heads_low, [kv_own, kv_other], 2 * kv_own.shape[2])
    fc1_rows = columns(fc1_w)
    w_fc1 = row_gather(after(fc1_rows, squares, mixed))
    grad_in = jnp.concatenate(trade_in(cotangent, is_odd, sizes))
    text_half = jnp.concatenate(ordered(is_odd, *trade_in(text_states, is_odd, sizes)), axis=-1)
    text_other = lax.ppermute(text_half, "dp", pair)
    text_in = jnp.concatenate(ordered(core == 1, text_half, text_other), axis=-1)
    text_count = text_in.shape[0]
    text_in = jnp.pad(text_in, ((0, -text_count % 128), (0, 0)))
    text_in = after(text_in, fc1_rows)
    text_kv = project_back_turned(text_in, w_kv2) + kv2_b[:, None]
    text_low = text_heads(text_kv, knorm2_gain).astype(jnp.bfloat16)
    mixed_low = after(mixed.reshape(model_width, -1).astype(jnp.bfloat16), text_low)
    resid_two = resid_one + project_sublanes(mixed_low, w_proj1) + proj1_b
    w_fc2 = row_gather(after(columns(fc2_w), w_fc1, resid_two))
    cross_in = layer_norm(resid_two, norm3_gain, norm3_bias).astype(jnp.bfloat16)
    cross_heads = project_turned(cross_in, w_q2) + q2_b[:, None]
    cross_heads = cross_heads.reshape(head_count, head_size, -1)
    cross_q = turn_heads(cross_heads, qnorm2_gain[None], qnorm2_bias[None], tables, head_count)
    cross_mixed, cross_log = attend(cross_q, [text_low], text_count)
    cross_low = cross_mixed.reshape(model_width, -1).astype(jnp.bfloat16)
    resid_three = resid_two + project_sublanes(cross_low, w_proj2) + proj2_b
    ffn_in = layer_norm(resid_three, norm2_gain, norm2_bias).astype(jnp.bfloat16)
    pre_act = project(ffn_in, w_fc1) + fc1_b
    hidden = gelu_tanh(pre_act).astype(jnp.bfloat16)
    block_low = (resid_three + project(hidden, w_fc2) + fc2_b).astype(jnp.bfloat16)
    block_out = trade_out(*jnp.split(block_low, 2), is_odd, sizes)

    scatter = partial(column_scatter, place=place, fsdp_size=fsdp_size)
    rows_fc2 = row_scatter(after(low_grad(hidden, grad_in), w_fc2))
    done_fc2 = scatter(rows_fc2)
    bias_fc2 = column_sum(grad_in)
    grad_hidden = project_back(grad_in, w_fc2)
    grad_pre = jax.vjp(gelu_tanh, pre_act)[1](grad_hidden)[0].astype(jnp.bfloat16)
    grad_fc1 = low_grad(ffn_in, grad_pre)
    bias_fc1 = column_sum(grad_pre)
    grad_ffn_in = project_back(grad_pre, w_fc1)
    grad_resid3, gain_n2, bias_n2 = jax.vjp(layer_norm, resid_three, norm2_gain, norm2_bias)[1](
        grad_ffn_in
    )
    grad_resid3 = grad_resid3 + grad_in.astype(jnp.float32)
    grad_branch2 = grad_resid3.astype(jnp.bfloat16)
    grad_proj2 = low_rows(cross_low, grad_branch2)
    bias_proj2 = column_sum(grad_branch2)
    grad_cross = project_back_turned(grad_branch2, w_proj2).reshape(head_count, head_size, -1)
    grad_cq, grad_ckv = attend_back(
        cross_q, grad_cross, cross_mixed, cross_log, [text_low], text_count, [jnp.float32]
    )
    grad_text, gain_kn2 = jax.vjp(text_heads, text_kv, knorm2_gain)[1](
        grad_ckv.reshape(2 * head_count, head_size, -1)
    )
    grad_text = grad_text.astype(jnp.bfloat16)
    grad_kv2 = low_rows(grad_text, text_in)
    bias_kv2 = jnp.sum(grad_text, axis=1, dtype=jnp.float32)
    text_back = project_sublanes(grad_text, w_kv2)[:text_count]
    text_mine, text_theirs = ordered(core == 1, *jnp.split(text_back, 2, axis=-1))
    text_mine = text_mine + lax.ppermute(text_theirs, "dp", pair)
    text_grad = trade_out(*ordered(is_odd, *jnp.split(text_mine, 2, axis=-1)), is_odd, sizes)
    grad_cproj, gain_qn2, bias_qn2 = turn_heads_back(
        cross_heads, grad_cq, [], qnorm2_gain[None], tables, head_count
    )
    gain_qn2, bias_qn2 = gain_qn2[0], bias_qn2[0]
    rows_fc1 = row_scatter(after(grad_fc1, rows_fc2, grad_cproj))
    done_fc1 = scatter(rows_fc1)
    grad_cproj = grad_cproj.reshape(model_width, -1).astype(jnp.bfloat16)
    grad_q2 = low_lanes(cross_in, grad_cproj)
    bias_q2 = jnp.sum(grad_cproj, axis=1, dtype=jnp.float32)
    grad_cross_in = back_sublanes(grad_cproj, w_q2)
    grad_resid2, gain_n3, bias_n3 = jax.vjp(layer_norm, resid_two, norm3_gain, norm3_bias)[1](
        grad_cross_in
    )
    grad_resid2 = grad_resid2 + grad_resid3
    grad_branch1 = grad_resid2.astype(jnp.bfloat16)
    grad_proj1 = low_rows(mixed_low, grad_branch1)
    bias_proj1 = column_sum(grad_branch1)
    grad_mixed = project_back_turned(grad_branch1, w_proj1).reshape(head_count, head_size, -1)
    grad_sq, grad_own, grad_other = attend_back(
        heads_low,
        grad_mixed,
        mixed,
        self_log,
        [kv_own, kv_other],
        2 * kv_own.shape[2],
        [jnp.float32, jnp.bfloat16],
    )
    grad_squares = jnp.stack([grad_proj1, grad_q2, grad_proj2])
    rows_square = lax.psum_scatter(
        after(grad_squares, rows_fc1, grad_sq, done_fc2, block_out), "dp", scatter_dimension=1, tiled=True
    )
    done_square = scatter(rows_square.reshape(-1, model_width))
    done_proj1, done_q2, done_proj2 = jnp.split(done_square, 3)
    kv_shape = kv_own.shape
    grad_taken = lax.ppermute(grad_other, "dp", pair).reshape(kv_shape)
    grad_qkv, self_gain, self_bias = turn_heads_back(
        qkv_heads,
        grad_sq,
        [grad_own.reshape(kv_shape), grad_taken],
        self_gains,
        tables,
        head_count,
    )
    gain_qn1, gain_kn1 = self_gain
    bias_qn1, bias_kn1 = self_bias
    grad_qkv = grad_qkv.reshape(3 * model_width, -1).astype(jnp.bfloat16)
    grad_qkv_w = low_lanes(normed, grad_qkv)
    bias_qkv = jnp.sum(grad_qkv, axis=1, dtype=jnp.float32)
    grad_normed = back_sublanes(grad_qkv, w_qkv)
    grad_shift = jnp.sum(grad_normed, axis=0)
    grad_resid1, gain_n1, bias_n1 = jax.vjp(layer_norm, resid_one, norm1_gain, norm1_bias)[1](
        grad_normed
    )
    grad_resid1 = (grad_resid1 + grad_resid2).astype(jnp.bfloat16)
    rows_qkv = row_scatter(after(grad_qkv_w, rows_square, grad_resid1, done_fc1))
    done_qkv = scatter(rows_qkv)
    grad_skip = low_grad(joined, grad_resid1)
    bias_skip = column_sum(grad_resid1)
    grad_joined = project_back(grad_resid1, w_skip)
    grad_cat, gain_skip, bias_skip_norm = jax.vjp(layer_norm, joined_in, skip_gain, skip_bias)[1](
        grad_joined
    )
    cat_low = grad_cat.astype(jnp.bfloat16)
    both_grad = trade_out(*jnp.split(cat_low, 2), is_odd, sizes)
    vectors = (
        gain_skip,
        bias_skip_norm,
        bias_skip,
        gain_n1,
        bias_n1,
        bias_qkv,
        gain_qn1,
        bias_qn1,
        gain_kn1,
        bias_kn1,
        bias_proj1,
        gain_n3,
        bias_n3,
        bias_q2,
        bias_kv2,
        gain_qn2,
        bias_qn2,
        gain_kn2,
        bias_proj2,
        gain_n2,
        bias_n2,
        bias_fc1,
        bias_fc2,
    )
    sequence = row_place // 2 * 4 + place
    spread_shift = jnp.where(
        jnp.arange(times.shape[0])[:, None] == sequence, grad_shift[None], 0.0
    )
    rows_skip = row_scatter(after(grad_skip, rows_qkv, done_square, cat_low, text_grad))
    done_skip = scatter(rows_skip)
    vector_rows = jnp.concatenate([spread_shift, pack_rows(vectors, model_width)])
    vector_rows = butterfly_sum(vector_rows, "dp", dp_size)
    vector_rows = butterfly_sum(after(vector_rows, both_grad), "fsdp", fsdp_size)
    shift_all = vector_rows[: times.shape[0]]
    summed = unpack_rows(vector_rows[times.shape[0] :], vectors)
    rows_kv2 = row_scatter(after(grad_kv2, rows_skip, done_qkv, vector_rows))
    done_kv2 = scatter(rows_kv2)
    ada_columns = ada_w.shape[1]
    grad_ada = lax.dot_general(
        embed_own.astype(jnp.float32),
        lax.dynamic_slice_in_dim(shift_all, place * ada_columns, ada_columns, 1),
        (((0,), (0,)), ((), ())),
        precision=lax.Precision.HIGHEST,
    )
    bias_ada = jnp.sum(shift_all, axis=0)
    return (
        block_out,
        both_grad[..., :model_width].astype(jnp.float32),
        both_grad[..., model_width:].astype(jnp.float32),
        text_grad,
        summed[0],
        summed[1],
        done_skip,
        summed[2],
        grad_ada,
        bias_ada,
        summed[3],
        summed[4],
        done_qkv,
        summed[5],
        summed[6],
        summed[7],
        summed[8],
        summed[9],
        done_proj1,
        summed[10],
        summed[11],
        summed[12],
        done_q2,
        summed[13],
        done_kv2,
        summed[14],
        summed[15],
        summed[16],
        summed[17],
        done_proj2,
        summed[18],
        summed[19],
        summed[20],
        done_fc1,
        summed[21],
        done_fc2,
        summed[22],
    )


def solution(mesh):
    in_specs = (
        P("dp", "fsdp", None),
        P("dp", "fsdp", None),
        P("dp", None, "fsdp"),
        P("dp"),
        P("dp", None, "fsdp"),
        P("dp", "fsdp", None),
        P(),
        P(),
        P("dp", "fsdp"),
        P(),
        P("dp", "fsdp"),
        P(),
        P(),
        P(),
        P("dp", "fsdp"),
        P(),
        P(),
        P(),
        P(),
        P(),
        P("dp", "fsdp"),
        P(),
        P(),
        P(),
        P("dp", "fsdp"),
        P(),
        P("dp", "fsdp"),
        P(),
        P(),
        P(),
        P(),
        P("dp", "fsdp"),
        P(),
        P(),
        P(),
        P("dp", "fsdp"),
        P(),
        P("dp", "fsdp"),
        P(),
    )
    out_specs = (
        P("dp", "fsdp", None),
        P("dp", "fsdp", None),
        P("dp", "fsdp", None),
        P("dp", None, "fsdp"),
        P(),
        P(),
        P("dp", "fsdp"),
        P(),
        P("dp", "fsdp"),
        P(),
        P(),
        P(),
        P("dp", "fsdp"),
        P(),
        P(),
        P(),
        P(),
        P(),
        P("dp", "fsdp"),
        P(),
        P(),
        P(),
        P("dp", "fsdp"),
        P(),
        P("dp", "fsdp"),
        P(),
        P(),
        P(),
        P(),
        P("dp", "fsdp"),
        P(),
        P(),
        P(),
        P("dp", "fsdp"),
        P(),
        P("dp", "fsdp"),
        P(),
    )
    return jax.shard_map(
        partial(body, mesh.shape["dp"], mesh.shape["fsdp"]),
        mesh=mesh,
        in_specs=in_specs,
        out_specs=out_specs,
        check_vma=False,
    )
```

time: 3210 us -> 1290 us (0.40)
  waiting for transfers between devices: 2360 us -> 556 us
  matrix products: 395 us -> 229 us
  blocking collectives: 121 us -> 0 us
  starting transfers between devices: 2.93 us -> 112 us
  Pallas kernels: 0 us -> 82.4 us
  other arithmetic: 155 us -> 93.7 us
    reduce_scatter x12 -> x6, waiting for transfers between devices: 1160 us -> 65.5 us  [the longest x5 65.5 us: row_scatter(): return lax.psum_scatter(gradient, 'dp', scatter_dimension=0, tiled=True)]
    all_gather x14 -> x6, waiting for transfers between devices: 561 us -> 58.5 us  [the longest x5 58.5 us: row_gather(): return lax.all_gather(rows, 'dp', axis=0, tiled=True)]
    ppermute x0 -> x55, waiting for transfers between devices: none -> 432 us  [the longest x7 85.8 us: column_gather(): other = lax.ppermute(shard, 'fsdp', swap_pairs(fsdp_size, 2))]
    psum x3 -> x0, waiting for transfers between devices: 429 us -> none  [the longest x1 262 us: body(): text_kv = lax.psum(text_part, 'fsdp') + kv2_b]
    unnamed x43 -> x12, waiting for transfers between devices: 215 us -> 0.2 us
    all_gather x5 -> x0, blocking collectives: 121 us -> none  [the longest x1 38 us: gather_columns(): lax.all_gather(matrices[0], 'fsdp', axis=1, tiled=True)]
    ppermute x0 -> x55, starting transfers between devices: none -> 111 us  [the longest x3 39 us: butterfly_gather(): other = lax.ppermute(values, axis_name, swap_pairs(size, step))]
    dot_general x67 -> x19, matrix products: 236 us -> 129 us  [the longest x3 40.6 us: low_grad(): lax.dot_general(inputs, grad_low, (((0,), (0,)), ((), ())), preferred_ele...]
  transfers between devices with their start and end apart: 36 -> 67, of which waited for: 34 -> 42; matrix products, arithmetic and copies ran while one was open for 14% -> 32% of each run, Pallas kernels for 0% -> 6%
where the time goes in v1:
time: 1290 us; the launch traced here: 1280 us
  waiting for transfers between devices  556 us (43%)
  matrix products  229 us (18%)
  local copies, waits for them, and re-layouts  160 us (12%)
  starting transfers between devices  112 us (9%)
  other arithmetic  93.7 us (7%)
  Pallas kernels  82.4 us (6%)
  between operations  47.2 us (4%)
    ppermute x7, waiting for transfers between devices, column_gather(): other = lax.ppermute(shard, 'fsdp', swap_pairs(fsdp_size, 2))  85.8 us
    ppermute x14, waiting for transfers between devices, trade(): lax.ppermute(part, ('dp', 'fsdp'), token_routes(dp_size, fsdp_size, flip))  79.8 us
    ppermute x7, waiting for transfers between devices, column_gather(): other = lax.ppermute(held, 'fsdp', swap_pairs(fsdp_size, 1))  78.6 us
    ppermute x6, waiting for transfers between devices, column_scatter(): lax.ppermute(given.astype(jnp.bfloat16), 'fsdp', swap_pairs(fsdp_size, 2))  74.4 us
    reduce_scatter x5, waiting for transfers between devices, row_scatter(): return lax.psum_scatter(gradient, 'dp', scatter_dimension=0, tiled=True)  65.5 us
    ppermute x8, waiting for transfers between devices, butterfly_sum(): values = values + lax.ppermute(values, axis_name, swap_pairs(size, step))  59.4 us
    all_gather x5, waiting for transfers between devices, row_gather(): return lax.all_gather(rows, 'dp', axis=0, tiled=True)  58.5 us
    dot_general x3, matrix products, project_back(): lax.dot_general(grad_low, weight, (((grad_low.ndim - 1,), (1,)), ((), ())...  54.1 us
  transfers between devices with their start and end apart: 67, of which 42 were waited for; matrix products, arithmetic and copies ran while one was open for 32% of the time, Pallas kernels for 6%

profile of v1, /device:TPU:0, one launch (start us, length us, event | category | flops | bytes accessed | tf_op | source)
XLA Modules:
  0.0 1280.5 jit_solution(1770893184261822286)
XLA Ops:
  43.6 17.7 %collective-permute-done.10 = bf16[176,1056]{1,0:T(8,128)(2,1)S(1)} collective-permute-done((bf16[176,1056]{1,0:T(8,128)(2,1)S(1)}, bf16[176,1056]{1,0:T(8,128)(2,1)S(1)}, u32[]{:S(2)}, u32[]{:S(2)}) %collective-permute-start.10) | collective-permute-done | bytes 371744 | tf_op jit(solution)/shard_map/ppermute | solution.py:358
  62.2 18.4 %collective-permute-done.11 = bf16[2,176,1056]{2,1,0:T(8,128)(2,1)S(1)} collective-permute-done((bf16[2,176,1056]{2,1,0:T(8,128)(2,1)S(1)}, bf16[2,176,1056]{2,1,0:T(8,128)(2,1)S(1)}, u32[]{:S(2)}, u32[]{:S(2)}) %collective-permute-start.11) | collective-permute-done | bytes 743456 | tf_op jit(solution)/shard_map/ppermute | solution.py:360
  120.8 47.1 %all-gather.9.cloned.1.call-done = bf16[1408,4224]{1,0:T(8,128)(2,1)} async-done(((bf16[176,4224]{1,0:T(8,128)(2,1)}), bf16[1408,4224]{1,0:T(8,128)(2,1)}) %all-gather.9.cloned.1.call-update) | async-done | bytes 11894800 | tf_op jit(solution)/shard_map/all_gather | solution.py:378
  174.0 18.7 %collective-permute-done.2 = bf16[528,352]{1,0:T(8,128)(2,1)S(1)} collective-permute-done((bf16[528,352]{1,0:T(8,128)(2,1)S(1)}, bf16[528,352]{1,0:T(8,128)(2,1)S(1)}, u32[]{:S(2)}, u32[]{:S(2)}) %collective-permute-start.2) | collective-permute-done | bytes 371744 | tf_op jit(solution)/shard_map/ppermute | solution.py:358
  197.6 14.9 %collective-permute-done.3 = bf16[2,528,352]{2,1,0:T(8,128)(2,1)S(1)} collective-permute-done((bf16[2,528,352]{2,1,0:T(8,128)(2,1)S(1)}, bf16[2,528,352]{2,1,0:T(8,128)(2,1)S(1)}, u32[]{:S(2)}, u32[]{:S(2)}) %collective-permute-start.3) | collective-permute-done | bytes 743456 | tf_op jit(solution)/shard_map/ppermute | solution.py:360
  224.9 25.9 %collective-permute-done.5 = bf16[256,2816]{1,0:T(8,128)(2,1)S(1)} collective-permute-done((bf16[256,2816]{1,0:T(8,128)(2,1)}, bf16[256,2816]{1,0:T(8,128)(2,1)S(1)}, u32[]{:S(2)}, u32[]{:S(2)}) %collective-permute-start.5) | collective-permute-done | bytes 1441824 | tf_op jit(solution)/shard_map/ppermute | solution.py:340
  264.6 36.5 %collective-permute-start.12 = (s32[2]{0:T(128)S(1)}, s32[2]{0:T(128)S(1)}, u32[]{:S(2)}, u32[]{:S(2)}) collective-permute-start(s32[2]{0:T(128)S(1)} %copy-done.158), channel_id=1, source_target_pairs={{0,4},{4,0},{8,12},{12,8},{16,20},{20,16},{24,28},{28,24},{1,5},{5... | collective-permute-start | bytes 32 | tf_op jit(solution)/shard_map/ppermute | solution.py:388
  388.5 22.3 %collective-permute-done.26 = bf16[768,352]{0,1:T(8,128)(2,1)} collective-permute-done((bf16[768,352]{0,1:T(8,128)(2,1)}, bf16[768,352]{0,1:T(8,128)(2,1)}, u32[]{:S(2)}, u32[]{:S(2)}) %collective-permute-start.26) | collective-permute-done | bytes 540704 | tf_op jit(solution)/shard_map/ppermute | solution.py:358
  424.4 19.8 %collective-permute-done.27 = bf16[2,768,352]{1,2,0:T(8,128)(2,1)} collective-permute-done((bf16[2,768,352]{1,2,0:T(8,128)(2,1)}, bf16[2,768,352]{1,2,0:T(8,128)(2,1)}, u32[]{:S(2)}, u32[]{:S(2)}) %collective-permute-start.27) | collective-permute-done | bytes 1081376 | tf_op jit(solution)/shard_map/ppermute | solution.py:360
  502.4 23.0 %collective-permute-done.31 = bf16[256,1408]{1,0:T(8,128)(2,1)} collective-permute-done((bf16[256,1408]{1,0:T(8,128)(2,1)}, bf16[256,1408]{1,0:T(8,128)(2,1)}, u32[]{:S(2)}, u32[]{:S(2)}) %collective-permute-start.31) | collective-permute-done | bytes 720928 | tf_op jit(solution)/shard_map/ppermute | solution.py:340
  555.5 17.0 %fusion.78 = f32[512,6144]{1,0:T(8,128)} fusion(bf16[1408,6144]{1,0:T(8,128)(2,1)} %all-gather.15.cloned.1.call-done, f32[512,1408]{1,0:T(8,128)S(1)} %get-tuple-element.559, f32[1408]{0:T(1024)S(1)} %copy-done.168, f32[1408]{0:T(1024)S(1)} %copy-done.144, f32[512]{0:T(512)S(1)} %fusion.70, f32[512]{0:T(512)S(1)} %broadcast_multiply_fusion.1), kind=kOutput, calls=%fused_computation.360 | convolution fusion | flops 8861974528 | bytes 32783360 | tf_op jit(solution)/shard_map/dot_general | solution.py:41
  572.4 19.3 %convolution_convert_fusion.1 = bf16[6144,1408]{1,0:T(8,128)(2,1)} fusion(bf16[512,1408]{1,0:T(8,128)(2,1)S(1)} %constant_dynamic-update-slice_fusion.5, f32[512,6144]{1,0:T(8,128)} %fusion.78, f32[6144]{0:T(1024)S(1)} %copy-done.163), kind=kOutput, calls=%fused_computation.1 | convolution fusion | flops 8898478080 | bytes 31350784 | tf_op jit(solution)/shard_map/dot_general | solution.py:446
  602.5 26.8 %convert_reduce_fusion = (f32[6144]{0:T(1024)}, bf16[512,6144]{1,0:T(8,128)(2,1)}) fusion(f32[512,6144]{1,0:T(8,128)} %fusion.78, f32[6144]{0:T(1024)S(1)} %copy-done.163, bf16[512,1408]{1,0:T(8,128)(2,1)} %copy-done.50, bf16[6144,1408]{1,0:T(8,128)(2,1)} %all-gather.17.cloned.1.call-done), kind=kOutput, calls=%fused_computation.12 | convolution fusion | flops 8930715648 | bytes 37666816 | tf_op jit(solution)/shard_map/dot_general | solution.py:45
  629.3 16.4 %convolution_convert_fusion = bf16[1408,6144]{1,0:T(8,128)(2,1)} fusion(bf16[512,6144]{1,0:T(8,128)(2,1)} %get-tuple-element.384, f32[512,1408]{1,0:T(8,128)} %copy-done.37, f32[1408]{0:T(1024)S(1)} %copy-done.168, f32[1408]{0:T(1024)S(1)} %copy-done.144, f32[512]{0:T(512)S(1)} %fusion.70, f32[512]{0:T(512)S(1)} %broadcast_multiply_fusion.1), kind=kOutput, calls=%fused_computation | convolution fusion | flops 8870625280 | bytes 26491904 | tf_op jit(solution)/shard_map/dot_general | solution.py:446
  646.9 19.2 %multiply_reduce_fusion = (f32[1408]{0:T(1024)}, f32[512]{0:T(512)S(1)}, f32[1408]{0:T(1024)}, f32[512,1408]{1,0:T(8,128)}) fusion(f32[512,1408]{1,0:T(8,128)} %copy-done.37, f32[512]{0:T(512)S(1)} %fusion.70, f32[512]{0:T(512)S(1)} %broadcast_multiply_fusion.1, f32[1408]{0:T(1024)S(1)} %copy-done.144, bf16[512,6144]{1,0:T(8,128)(2,1)} %get-tuple-element.384, ...), kind=kOutput, calls=%fused_computation.69 | convolution fusion | flops 8864134144 | bytes 29383168 | tf_op jit(solution)/shard_map/dot_general | solution.py:45
  697.5 20.4 %reduce-scatter.7.cloned.1.call-done = bf16[768,1408]{1,0:T(8,128)(2,1)} async-done(((bf16[6144,1408]{1,0:T(8,128)(2,1)}), bf16[768,1408]{1,0:T(8,128)(2,1)}) %reduce-scatter.7.cloned.1.call-update) | async-done | bytes 2162704 | tf_op jit(solution)/shard_map/reduce_scatter | solution.py:382
  723.1 21.4 %fusion.41 = bf16[512,1408]{1,0:T(8,128)(2,1)S(1)} fusion(f32[512,1408]{1,0:T(8,128)} %copy-done.37, bf16[6144,1408]{1,0:T(8,128)(2,1)} %all-gather.17.cloned.1.call-done, f32[1408]{0:T(1024)S(1)} %copy-done.169, f32[512,6144]{1,0:T(8,128)} %fusion.78, f32[6144]{0:T(1024)S(1)} %copy-done.163), kind=kOutput, calls=%fused_computation.64 | convolution fusion | flops 8891990016 | bytes 34240000 | tf_op jit(solution)/shard_map/dot_general | solution.py:41
  790.3 27.3 %shard_map.660 = (f32[16,88,512]{2,1,0:T(8,128)S(1)}, f32[2,16,88,512]{3,2,1,0:T(8,128)}, bf16[2,16,88,512]{3,2,1,0:T(8,128)(2,1)S(1)}) custom-call(bf16[48,88,512]{2,1,0:T(8,128)(2,1)} %copy-done.6, f32[16,88,512]{2,1,0:T(8,128)S(1)} %fusion.49.grad_ref, f32[16,88,512]{2,1,0:T(8,128)S(1)} %get-tuple-element.232.mixed_ref, ...), custom_call_target="tpu_custom_call" | custom-call | flops 7381975040 | bytes 17301504 | tf_op jit(solution)/shard_map/pallas_call | solution.py:304
  830.3 22.9 %collective-permute-done.44 = bf16[768,352]{0,1:T(8,128)(2,1)} collective-permute-done((bf16[768,352]{0,1:T(8,128)(2,1)}, bf16[768,352]{0,1:T(8,128)(2,1)}, u32[]{:S(2)}, u32[]{:S(2)}) %collective-permute-start.44) | collective-permute-done | bytes 540704 | tf_op jit(solution)/shard_map/ppermute | solution.py:373
  941.0 24.2 %collective-permute-done.46 = bf16[176,1536]{1,0:T(8,128)(2,1)S(1)} collective-permute-done((bf16[176,1536]{1,0:T(8,128)(2,1)S(1)}, bf16[176,1536]{1,0:T(8,128)(2,1)S(1)}, u32[]{:S(2)}, u32[]{:S(2)}) %collective-permute-start.46) | collective-permute-done | bytes 540704 | tf_op jit(solution)/shard_map/ppermute | solution.py:373
  1016.5 15.8 %collective-permute-done.47 = bf16[2,528,352]{2,1,0:T(8,128)(2,1)S(1)} collective-permute-done((bf16[2,528,352]{2,1,0:T(8,128)(2,1)S(1)}, bf16[2,528,352]{2,1,0:T(8,128)(2,1)S(1)}, u32[]{:S(2)}, u32[]{:S(2)}) %collective-permute-start.47) | collective-permute-done | bytes 743456 | tf_op jit(solution)/shard_map/ppermute | solution.py:370
  1092.8 20.6 %collective-permute-done.33 = bf16[256,2816]{1,0:T(8,128)(2,1)S(1)} collective-permute-done((bf16[256,2816]{1,0:T(8,128)(2,1)S(1)}, bf16[256,2816]{1,0:T(8,128)(2,1)S(1)}, u32[]{:S(2)}, u32[]{:S(2)}) %collective-permute-start.33) | collective-permute-done | bytes 1441824 | tf_op jit(solution)/shard_map/ppermute | solution.py:340
  1116.9 25.7 %collective-permute-done.41 = f32[48,1408]{1,0:T(8,128)S(1)} collective-permute-done((f32[48,1408]{1,0:T(8,128)}, f32[48,1408]{1,0:T(8,128)S(1)}, u32[]{:S(2)}, u32[]{:S(2)}) %collective-permute-start.41) | collective-permute-done | bytes 270368 | tf_op jit(solution)/shard_map/ppermute | solution.py:397
  1205.4 39.3 %reduce-scatter.17.cloned.1.call-done = bf16[352,1024]{1,0:T(8,128)(2,1)} async-done(((bf16[2816,1024]{1,0:T(8,128)(2,1)}), bf16[352,1024]{1,0:T(8,128)(2,1)}) %reduce-scatter.17.cloned.1.call-update) | async-done | bytes 720912 | tf_op jit(solution)/shard_map/reduce_scatter | solution.py:382
  (801 shorter events, 672.9 us)
Async XLA Ops:
  7.2 87.6 %all-gather.7.cloned.1.call-start = ((), (), s32[]{:S(2)}) async-start(), calls=%async_computation.6 | async-start | bytes 8921088 | tf_op jit(solution)/shard_map/all_gather | solution.py:378
  40.3 127.6 %all-gather.9.cloned.1.call-start = ((), (), s32[]{:S(2)}) async-start(), calls=%async_computation.7 | async-start | bytes 13381632 | tf_op jit(solution)/shard_map/all_gather | solution.py:378
  98.6 159.9 %all-gather.11.cloned.1.call-start = ((), (), s32[]{:S(2)}) async-start(), calls=%async_computation.8 | async-start | bytes 6488064 | tf_op jit(solution)/shard_map/all_gather | solution.py:378
  171.3 204.1 %all-gather.13.cloned.1.call-start = ((), (), s32[]{:S(2)}) async-start(), calls=%async_computation.9 | async-start | bytes 13381632 | tf_op jit(solution)/shard_map/all_gather | solution.py:530
  218.1 32.8 %collective-permute-start.5 = (bf16[256,2816]{1,0:T(8,128)(2,1)}, bf16[256,2816]{1,0:T(8,128)(2,1)S(1)}, u32[]{:S(2)}, u32[]{:S(2)}) collective-permute-start(bf16[256,2816]{1,0:T(8,128)(2,1)} %get-tuple-element.414), channel_id=1, source_target_pairs={{0,1},{1,0},{2,5},{3,4},{4,3},{5,2},{6,7},{7,6},{8,9},{9,8},{10,13... | collective-permute-start | bytes 4325384 | tf_op jit(solution)/shard_map/ppermute | solution.py:340
  262.9 223.4 %all-gather.15.cloned.1.call-start = ((), (), s32[]{:S(2)}) async-start(), calls=%async_computation.10 | async-start | bytes 19464192 | tf_op jit(solution)/shard_map/all_gather | solution.py:378
  262.9 48.2 %collective-permute-start.8 = (s32[2,256]{1,0:T(2,128)S(1)}, s32[2,256]{1,0:T(2,128)S(1)}, u32[]{:S(2)}, u32[]{:S(2)}) collective-permute-start(s32[2,256]{1,0:T(2,128)S(1)} %get-tuple-element.534), channel_id=1, source_target_pairs={{0,0},{1,1},{2,4},{3,5},{4,2},{5,3},{6,6},{7,7},{8,8},{9,9},{10,12... | collective-permute-start | bytes 6152 | tf_op jit(solution)/shard_map/ppermute | solution.py:340
  263.8 50.0 %collective-permute-start.9 = (s32[2,256]{1,0:T(2,128)S(1)}, s32[2,256]{1,0:T(2,128)S(1)}, u32[]{:S(2)}, u32[]{:S(2)}) collective-permute-start(s32[2,256]{1,0:T(2,128)S(1)} %get-tuple-element.533), channel_id=1, source_target_pairs={{0,1},{1,0},{2,5},{3,4},{4,3},{5,2},{6,7},{7,6},{8,9},{9,8},{10,13... | collective-permute-start | bytes 6152 | tf_op jit(solution)/shard_map/ppermute | solution.py:340
  264.6 38.5 %collective-permute-start.12 = (s32[2]{0:T(128)S(1)}, s32[2]{0:T(128)S(1)}, u32[]{:S(2)}, u32[]{:S(2)}) collective-permute-start(s32[2]{0:T(128)S(1)} %copy-done.158), channel_id=1, source_target_pairs={{0,4},{4,0},{8,12},{12,8},{16,20},{20,16},{24,28},{28,24},{1,5},{5... | collective-permute-start | bytes 32 | tf_op jit(solution)/shard_map/ppermute | solution.py:388
  379.9 213.0 %all-gather.17.cloned.1.call-start = ((), (), s32[]{:S(2)}) async-start(), calls=%async_computation.11 | async-start | bytes 19464192 | tf_op jit(solution)/shard_map/all_gather | solution.py:378
  384.6 34.3 %collective-permute-start.21 = (bf16[333,256]{1,0:T(8,128)(2,1)}, bf16[333,256]{1,0:T(8,128)(2,1)}, u32[]{:S(2)}, u32[]{:S(2)}) collective-permute-start(bf16[333,256]{1,0:T(8,128)(2,1)} %get-tuple-element.491), channel_id=1, source_target_pairs={{0,1},{1,0},{2,5},{3,4},{4,3},{5,2},{6,7},{7,6},{8,9},{9,8},{10,13... | collective-permute-start | bytes 511496 | tf_op jit(solution)/shard_map/ppermute | solution.py:340
  384.6 34.3 %collective-permute-start.22 = (bf16[333,256]{1,0:T(8,128)(2,1)S(1)}, bf16[333,256]{1,0:T(8,128)(2,1)}, u32[]{:S(2)}, u32[]{:S(2)}) collective-permute-start(bf16[333,256]{1,0:T(8,128)(2,1)S(1)} %get-tuple-element.492), channel_id=1, source_target_pairs={{0,0},{1,1},{2,4},{3,5},{4,2},{5,3},{6,6},{7,7},{8,8},{9,9},{10,12... | collective-permute-start | bytes 511496 | tf_op jit(solution)/shard_map/ppermute | solution.py:340
  490.7 227.3 %reduce-scatter.7.cloned.1.call-start = ((), (), s32[]{:S(2)}) async-start(), calls=%async_computation.12 | async-start | bytes 19464192 | tf_op jit(solution)/shard_map/reduce_scatter | solution.py:382
  596.7 261.4 %reduce-scatter.9.cloned.1.call-start = ((), (), s32[]{:S(2)}) async-start(), calls=%async_computation.13 | async-start | bytes 19464192 | tf_op jit(solution)/shard_map/reduce_scatter | solution.py:382
  722.4 244.5 %reduce-scatter.11.cloned.1.call-start = ((), (), s32[]{:S(2)}) async-start(), calls=%async_computation.14 | async-start | bytes 13381632 | tf_op jit(solution)/shard_map/reduce_scatter | solution.py:626
  745.7 81.8 %collective-permute-start.28 = (bf16[256,1408]{1,0:T(8,128)(2,1)}, bf16[256,1408]{1,0:T(8,128)(2,1)}, u32[]{:S(2)}, u32[]{:S(2)}) collective-permute-start(bf16[256,1408]{1,0:T(8,128)(2,1)} %get-tuple-element.444), channel_id=1, source_target_pairs={{0,1},{1,0},{2,5},{3,4},{4,3},{5,2},{6,7},{7,6},{8,9},{9,8},{10,13... | collective-permute-start | bytes 2162696 | tf_op jit(solution)/shard_map/ppermute | solution.py:340
  747.0 80.4 %collective-permute-start.29 = (bf16[256,1408]{1,0:T(8,128)(2,1)}, bf16[256,1408]{1,0:T(8,128)(2,1)}, u32[]{:S(2)}, u32[]{:S(2)}) collective-permute-start(bf16[256,1408]{1,0:T(8,128)(2,1)} %get-tuple-element.445), channel_id=1, source_target_pairs={{0,0},{1,1},{2,4},{3,5},{4,2},{5,3},{6,6},{7,7},{8,8},{9,9},{10,12... | collective-permute-start | bytes 2162696 | tf_op jit(solution)/shard_map/ppermute | solution.py:340
  783.1 38.2 %collective-permute-start.43 = (bf16[2,768,352]{1,2,0:T(8,128)(2,1)}, bf16[2,768,352]{1,2,0:T(8,128)(2,1)}, u32[]{:S(2)}, u32[]{:S(2)}) collective-permute-start(bf16[2,768,352]{1,2,0:T(8,128)(2,1)} %copy.114), channel_id=1, source_target_pairs={{0,1},{1,0},{2,3},{3,2},{4,5},{5,4},{6,7},{7,6},{8,9},{9,8},{10,11... | collective-permute-start | bytes 3244040 | tf_op jit(solution)/shard_map/ppermute | solution.py:370
  863.8 197.5 %reduce-scatter.13.cloned.1.call-start = ((), (), s32[]{:S(2)}) async-start(), calls=%async_computation.15 | async-start | bytes 13381632 | tf_op jit(solution)/shard_map/reduce_scatter | solution.py:382
  972.0 210.5 %reduce-scatter.15.cloned.1.call-start = ((), (), s32[]{:S(2)}) async-start(), calls=%async_computation.16 | async-start | bytes 8921088 | tf_op jit(solution)/shard_map/reduce_scatter | solution.py:382
  1067.1 177.6 %reduce-scatter.17.cloned.1.call-start = ((), (), s32[]{:S(2)}) async-start(), calls=%async_computation.17 | async-start | bytes 6488064 | tf_op jit(solution)/shard_map/reduce_scatter | solution.py:382
  1072.3 41.0 %collective-permute-start.33 = (bf16[256,2816]{1,0:T(8,128)(2,1)S(1)}, bf16[256,2816]{1,0:T(8,128)(2,1)S(1)}, u32[]{:S(2)}, u32[]{:S(2)}) collective-permute-start(bf16[256,2816]{1,0:T(8,128)(2,1)S(1)} %get-tuple-element.412), channel_id=1, source_target_pairs={{0,1},{1,0},{2,5},{3,4},{4,3},{5,2},{6,7},{7,6},{8,9},{9,8},{10,13... | collective-permute-start | bytes 4325384 | tf_op jit(solution)/shard_map/ppermute | solution.py:340
  1091.3 61.5 %collective-permute-start.51 = (bf16[2,176,1056]{2,1,0:T(8,128)(2,1)}, bf16[2,176,1056]{2,1,0:T(8,128)(2,1)}, u32[]{:S(2)}, u32[]{:S(2)}) collective-permute-start(bf16[2,176,1056]{2,1,0:T(8,128)(2,1)} %broadcast_select_fusion.6), channel_id=1, source_target_pairs={{0,1},{1,0},{2,3},{3,2},{4,5},{5,4},{6,7},{7,6},{8,9},{9,8},{10,11... | collective-permute-start | bytes 2230280 | tf_op jit(solution)/shard_map/ppermute | solution.py:370
  1204.4 43.2 %collective-permute-start.49 = (bf16[2,352,352]{2,1,0:T(8,128)(2,1)S(1)}, bf16[2,352,352]{2,1,0:T(8,128)(2,1)S(1)}, u32[]{:S(2)}, u32[]{:S(2)}) collective-permute-start(bf16[2,352,352]{2,1,0:T(8,128)(2,1)S(1)} %broadcast_select_fusion.12), channel_id=1, source_target_pairs={{0,1},{1,0},{2,3},{3,2},{4,5},{5,4},{6,7},{7,6},{8,9},{9,8},{10,11... | collective-permute-start | bytes 1486856 | tf_op jit(solution)/shard_map/ppermute | solution.py:370
  (219 other events, 3413.0 us)
Sparse Core Ops, SparseCore 0:
  40.5 54.3 all-gather.6
  98.7 69.2 all-gather.8
  171.5 43.3 all-gather.10
  263.0 102.2 all-gather.12
  380.0 90.8 all-gather.14
  490.8 90.4 all-gather.16
  596.8 121.1 reduce-scatter.6
  722.5 118.6 reduce-scatter.8
  863.9 88.6 reduce-scatter.10
  972.1 89.1 reduce-scatter.12
  1067.2 69.0 reduce-scatter.14
  1187.7 56.8 reduce-scatter.16
